TPU v7x, 32 devices: a whole 2x2x4 slice. The times are simulated.
32 devices in a mesh: seq: 8 (over z, x), head: 4 (over y, core).
Axes of the slice: x: 2, y: 2, z: 4, core: 2. Of those that a mesh axis runs over, the one named last changes fastest.
Arguments:
- query: bfloat16 [4096, 4096], P(('seq', 'head')), may hold values from -41 to 41
- keys: bfloat16 [131072, 1024], P('seq', 'head'), may hold values from -14 to 14
- values: bfloat16 [131072, 1024], P('seq', 'head'), may hold values from -6 to 6
- out_grad: bfloat16 [4096, 4096], P(('seq', 'head')), may hold values from -6 to 6
- span_pos: int32 [8], P('seq'), may hold values from 1 to 31, as said below
- selected: int32 [8, 4], P('seq'), may hold values from -1 to 254, as said below
Outputs:
- attn_out: bfloat16 [4096, 4096], P(('seq', 'head'))
- query_grad: bfloat16 [4096, 4096], P(('seq', 'head'))
- key_grad: bfloat16 [131072, 1024], P('seq', 'head')
- value_grad: bfloat16 [131072, 1024], P('seq', 'head')
Inputs may be any that keep to these rules, and one draw needn't show every extreme that they name: `span_pos`: block index of the span's queries within its shard. `selected`: entry [s, j] is -1 if s < j; otherwise it indexes a block of shard s - j (blocks (s - j) * 32 onward), and for j = 0 one earlier than span s's own block s * 32 + span_pos[s].
All inputs are finite; a program needn't handle non-finite values.
Results may differ from a plain program's by a relative error of at most 0.029.
Values may be sent and summed in bfloat16 or wider, within the bound.
No kernel may reach another device: no remote copies, remote signals or barrier semaphores. Data moves between devices by JAX's collectives and lax.ppermute only.
A program may use at most 192 MiB of HBM per device.

v0:
```python
import functools
import math

import jax
import jax.numpy as jnp
from jax import lax
from jax.experimental import pallas as pl
from jax.experimental.pallas import tpu as pltpu
from jax.sharding import PartitionSpec as P

HEAD_DIM = 128
MASKED = -1e30
VMEM_LIMIT = 48 << 20

ROWS_ROWS = (((1,), (1,)), ((), ()))
ROWS_COLS = (((1,), (0,)), ((), ()))
HBM = pl.BlockSpec(memory_space=pl.ANY)
SMEM = pl.BlockSpec(memory_space=pltpu.SMEM)
VMEM = pl.BlockSpec(memory_space=pltpu.VMEM)


def shifted(value, axis, steps):
    count = lax.axis_size(axis)
    first, last = (max(0, -steps), min(count, count - steps))
    return lax.ppermute(value, axis, [(source, source + steps) for source in range(first, last)])


def flipped(value, axis, mask):
    count = lax.axis_size(axis)
    return lax.ppermute(value, axis, [(source, source ^ mask) for source in range(count)])


def dot(left, right, dims):
    return lax.dot_general(left, right, dims, preferred_element_type=jnp.float32)


def split_queries(query, out_grad, me, heads):
    rows, width = query.shape
    count = lax.axis_size("head")
    part = width // (count * heads)

    def kernel(me_ref, q_ref, g_ref, *outs):
        for head in range(heads):
            for r in range(count):
                start = pl.multiple_of((me_ref[0] ^ r) * heads * part + head * part, 128)
                outs[head * count + r][0] = q_ref[:, pl.ds(start, part)]
                outs[head * count + r][1] = g_ref[:, pl.ds(start, part)]

    flat = pl.pallas_call(
        kernel,
        in_specs=[SMEM, VMEM, VMEM],
        out_specs=[VMEM] * (heads * count),
        out_shape=[jax.ShapeDtypeStruct((2, rows, part), query.dtype)] * (heads * count),
        compiler_params=pltpu.CompilerParams(vmem_limit_bytes=VMEM_LIMIT),
        name="split_queries",
    )(me, query, out_grad)
    return [flat[head * count : (head + 1) * count] for head in range(heads)]


def gather_blocks(keys, values, wanted, seq_index, block_rows, heads):
    shard_blocks = keys.shape[0] // block_rows
    count = len(wanted)

    def kernel(seq_ref, *refs):
        entries = refs[:count]
        k_ref, v_ref = refs[count : count + 2]
        outs = refs[count + 2 : -1]
        sem = refs[-1]
        copies = []
        for head in range(heads):
            for d in range(count):
                local = entries[d][0, d + 1] - seq_ref[0] * shard_blocks
                local = jnp.clip(local, 0, shard_blocks - 1)
                rows = pl.ds(pl.multiple_of(local * block_rows, block_rows), block_rows)
                cols = pl.ds(head * HEAD_DIM, HEAD_DIM)
                for which, source in enumerate((k_ref, v_ref)):
                    slot = (head * count + d) * 2 + which
                    copies.append(
                        pltpu.make_async_copy(
                            source.at[rows, cols], outs[head * count + d].at[which], sem.at[slot]
                        )
                    )
        for copy in copies:
            copy.start()
        for copy in copies:
            copy.wait()

    flat = pl.pallas_call(
        kernel,
        in_specs=[SMEM] * (1 + count) + [HBM, HBM],
        out_specs=[VMEM] * (heads * count),
        out_shape=[jax.ShapeDtypeStruct((2, block_rows, HEAD_DIM), keys.dtype)] * (heads * count),
        scratch_shapes=[pltpu.SemaphoreType.DMA((heads * count * 2,))],
        compiler_params=pltpu.CompilerParams(vmem_limit_bytes=VMEM_LIMIT),
        name="gather_blocks",
    )(seq_index, *wanted, keys, values)
    return [flat[head * count : (head + 1) * count] for head in range(heads)]


def attend(me, chosen, span_pos, pieces, keys, values, arrived, head):
    count = len(pieces)
    rows = pieces[0].shape[1]
    group = pieces[0].shape[2] // HEAD_DIM
    block = count * rows
    picks = chosen.shape[1]
    slots = picks + 1
    shard_blocks = keys.shape[0] // block
    scale = HEAD_DIM**-0.5
    log2e = math.log2(math.e)
    fresh = 2 if head == 0 else 0
    clear_rows = math.gcd(keys.shape[0], 2048)
    clear_steps = keys.shape[0] // clear_rows
    clear_scratch = []
    if fresh:
        clear_scratch.append(pltpu.VMEM((clear_rows, keys.shape[1]), keys.dtype))
        clear_scratch.append(pltpu.SemaphoreType.DMA((fresh * clear_steps,)))

    def kernel(me_ref, chosen_ref, pos_ref, *refs):
        piece_refs, refs = refs[:count], refs[count:]
        first_k, first_v, own_k, own_v = refs[:4]
        refs = refs[4:]
        arrived_refs, refs = refs[: picks - 1], refs[picks - 1 :]
        out_refs, refs = refs[:count], refs[count:]
        grad_refs, refs = refs[:slots], refs[slots:]
        zero_refs, refs = refs[:fresh], refs[fresh:]
        s_ref, acc_k, acc_v, k_t, v_t = refs[:5]
        key_refs = [first_k] + [ref.at[0] for ref in arrived_refs] + [own_k]
        value_refs = [first_v] + [ref.at[1] for ref in arrived_refs] + [own_v]
        spans = [slice(slot * block, (slot + 1) * block) for slot in range(slots)]
        step = pl.program_id(0)
        clears = []
        if fresh:
            blank, blank_sem = refs[5:]
            for which, target in enumerate(zero_refs):
                for part in range(clear_steps):
                    place = target.at[pl.ds(part * clear_rows, clear_rows)]
                    slot = blank_sem.at[which * clear_steps + part]
                    clears.append(pltpu.make_async_copy(blank, place, slot))

        @pl.when(step == 0)
        def _():
            if fresh:
                blank[...] = jnp.zeros_like(blank)
            for clear in clears:
                clear.start()
            for slot in range(slots):
                k_t[:, spans[slot]] = key_refs[slot][...].T
                v_t[:, spans[slot]] = value_refs[slot][...].T

        q = jnp.concatenate([ref[0] for ref in piece_refs], 0)
        g = jnp.concatenate([ref[1] for ref in piece_refs], 0)
        top = jnp.full((1, block), MASKED, jnp.float32)
        for slot in range(slots):
            s = dot(key_refs[slot][...], q, ROWS_ROWS) * (scale * log2e)
            if slot == picks:
                key_pos = lax.broadcasted_iota(jnp.int32, (block, block), 0)
                column = lax.broadcasted_iota(jnp.int32, (block, block), 1)
                query_pos = ((column // rows) ^ me_ref[0]) * rows + column % rows
                s = jnp.where(key_pos <= query_pos, s, MASKED)
            else:
                s = jnp.where(chosen_ref[0, slot] >= 0, s, MASKED)
            s_ref[spans[slot]] = s
            top = jnp.maximum(top, jnp.max(s, axis=0, keepdims=True))
        total = jnp.zeros((1, block), jnp.float32)
        for slot in range(slots):
            e = jnp.exp2(s_ref[spans[slot]] - top)
            s_ref[spans[slot]] = e
            total = total + jnp.sum(e, axis=0, keepdims=True)
        inverse = 1.0 / total
        o_t = jnp.zeros((HEAD_DIM, block), jnp.float32)
        for slot in range(slots):
            w = s_ref[spans[slot]] * inverse
            s_ref[spans[slot]] = w
            low = w.astype(jnp.bfloat16)
            o_t = o_t + dot(v_t[:, spans[slot]], low, ROWS_COLS)
            before = jnp.where(step == 0, 0.0, acc_v[spans[slot]])
            acc_v[spans[slot]] = before + dot(low, g, ROWS_COLS)
        o_t = o_t.astype(jnp.bfloat16).astype(jnp.float32)
        delta = jnp.sum(g.T.astype(jnp.float32) * o_t, axis=0, keepdims=True)
        q_t = jnp.zeros((HEAD_DIM, block), jnp.float32)
        for slot in range(slots):
            w_grad = dot(value_refs[slot][...], g, ROWS_ROWS)
            s_grad = (s_ref[spans[slot]] * (w_grad - delta)).astype(jnp.bfloat16)
            q_t = q_t + dot(k_t[:, spans[slot]], s_grad, ROWS_COLS)
            before = jnp.where(step == 0, 0.0, acc_k[spans[slot]])
            acc_k[spans[slot]] = before + dot(s_grad, q, ROWS_COLS)
        o = o_t.T.astype(jnp.bfloat16)
        q_grad = (q_t * scale).T.astype(jnp.bfloat16)
        for r in range(count):
            out_refs[r][0] = o[r * rows : (r + 1) * rows]
            out_refs[r][1] = q_grad[r * rows : (r + 1) * rows]

        @pl.when(step == group - 1)
        def _():
            for slot in range(slots):
                grad_refs[slot][0] = (acc_k[spans[slot]] * scale).astype(jnp.bfloat16)
                grad_refs[slot][1] = acc_v[spans[slot]].astype(jnp.bfloat16)
            for clear in clears:
                clear.wait()

    def first_index(step, me, chosen, pos):
        return (jnp.maximum(lax.rem(chosen[0, 0], shard_blocks), 0), head)

    def own_index(step, me, chosen, pos):
        return (pos[0], head)

    def whole_index(step, me, chosen, pos):
        return (0, 0, 0)

    piece = pl.BlockSpec((2, rows, HEAD_DIM), lambda step, me, chosen, pos: (0, 0, step))
    pair = pl.BlockSpec((2, block, HEAD_DIM), whole_index)
    flops = 12 * block * slots * block * HEAD_DIM * group
    result = pl.pallas_call(
        kernel,
        grid_spec=pltpu.PrefetchScalarGridSpec(
            num_scalar_prefetch=3,
            grid=(group,),
            in_specs=[piece] * count
            + [pl.BlockSpec((block, HEAD_DIM), first_index)] * 2
            + [pl.BlockSpec((block, HEAD_DIM), own_index)] * 2
            + [pair] * (picks - 1),
            out_specs=[piece] * count + [pair] * slots + [HBM] * fresh,
            scratch_shapes=[
                pltpu.VMEM((slots * block, block), jnp.float32),
                pltpu.VMEM((slots * block, HEAD_DIM), jnp.float32),
                pltpu.VMEM((slots * block, HEAD_DIM), jnp.float32),
                pltpu.VMEM((HEAD_DIM, slots * block), jnp.bfloat16),
                pltpu.VMEM((HEAD_DIM, slots * block), jnp.bfloat16),
            ]
            + clear_scratch,
        ),
        out_shape=[jax.ShapeDtypeStruct(pieces[0].shape, jnp.bfloat16)] * count
        + [jax.ShapeDtypeStruct((2, block, HEAD_DIM), jnp.bfloat16)] * slots
        + [jax.ShapeDtypeStruct(keys.shape, keys.dtype)] * fresh,
        compiler_params=pltpu.CompilerParams(vmem_limit_bytes=VMEM_LIMIT),
        cost_estimate=pl.CostEstimate(
            flops=flops, bytes_accessed=8 << 20, transcendentals=block * block * slots * group
        ),
        name="attend",
    )(me, chosen, span_pos, *pieces, keys, values, keys, values, *arrived)
    return (result[:count], result[count : count + slots], result[count + slots :])


def finish(ids, chosen, span_pos, wanted, outs, contributions, buffers, shapes, head, heads):
    count = len(outs)
    rows, part = outs[0].shape[1:]
    slots = len(contributions)
    picks = slots - 1
    block = contributions[0].shape[1]
    fresh = len(shapes) - len(buffers)

    def kernel(ids_ref, chosen_ref, pos_ref, *refs):
        wanted_refs, refs = refs[: picks - 1], refs[picks - 1 :]
        out_refs, refs = refs[:count], refs[count:]
        given, refs = refs[:slots], refs[slots:]
        refs = refs[len(buffers) :]
        attn_ref, query_ref, key_ref, value_ref = refs[:4]
        sums, out_sem, grad_sem = refs[4:]
        seq, me = ids_ref[0], ids_ref[1]
        shard_blocks = key_ref.shape[0] // block
        copies = []
        for r in range(count):
            start = pl.multiple_of((me ^ r) * heads * part + head * part, 128)
            for which, target in enumerate((attn_ref, query_ref)):
                copies.append(
                    pltpu.make_async_copy(
                        out_refs[r].at[which],
                        target.at[:, pl.ds(start, part)],
                        out_sem.at[r * 2 + which],
                    )
                )
        for copy in copies:
            copy.start()
        targets = [jnp.where(chosen_ref[0, 0] >= 0, chosen_ref[0, 0] - seq * shard_blocks, -1)]
        for d in range(1, picks):
            above = seq + d < lax.axis_size("seq")
            local = wanted_refs[d - 1][0, d] - seq * shard_blocks
            targets.append(jnp.where(above, local, -1))
        targets.append(pos_ref[0])
        present = [(t >= 0) & (t < shard_blocks) for t in targets]
        same = {}
        for i in range(slots):
            for j in range(i + 1, slots):
                same[i, j] = present[i] & (targets[i] == targets[j])

        def moves(i, source):
            start = pl.multiple_of(jnp.clip(targets[i], 0, shard_blocks - 1) * block, block)
            place = (pl.ds(start, block), pl.ds(head * HEAD_DIM, HEAD_DIM))
            return [
                pltpu.make_async_copy(source.at[which], target.at[place], grad_sem.at[i * 2 + which])
                for which, target in enumerate((key_ref, value_ref))
            ]

        leads = []
        for i in range(slots):
            lead = present[i]
            for j in range(i):
                lead = lead & jnp.logical_not(same[j, i])
            shared = jnp.bool_(False)
            for j in range(i + 1, slots):
                shared = shared | same[i, j]
            leads.append(lead)

            @pl.when(lead & jnp.logical_not(shared))
            def _(i=i):
                for copy in moves(i, given[i]):
                    copy.start()

            @pl.when(lead & shared)
            def _(i=i):
                value = given[i][...].astype(jnp.float32)
                for j in range(i + 1, slots):
                    value = value + jnp.where(same[i, j], given[j][...].astype(jnp.float32), 0.0)
                sums[i] = value.astype(jnp.bfloat16)
                for copy in moves(i, sums.at[i]):
                    copy.start()

        for i in range(slots):

            @pl.when(leads[i])
            def _(i=i):
                for copy in moves(i, given[i]):
                    copy.wait()

        for copy in copies:
            copy.wait()

    base = 3 + picks - 1 + count + slots
    return pl.pallas_call(
        kernel,
        in_specs=[SMEM] * (3 + picks - 1)
        + [VMEM] * count
        + [VMEM] * slots
        + [HBM] * len(buffers),
        out_specs=[HBM] * 4,
        out_shape=shapes,
        scratch_shapes=[
            pltpu.VMEM((slots, 2, block, HEAD_DIM), jnp.bfloat16),
            pltpu.SemaphoreType.DMA((count * 2,)),
            pltpu.SemaphoreType.DMA((slots * 2,)),
        ],
        input_output_aliases={base + i: fresh + i for i in range(len(buffers))},
        compiler_params=pltpu.CompilerParams(vmem_limit_bytes=VMEM_LIMIT),
        name="finish",
    )(ids, chosen, span_pos, *wanted, *outs, *contributions, *buffers)


def per_device(query, keys, values, out_grad, span_pos, selected):
    count = lax.axis_size("head")
    seq_index = lax.axis_index("seq").astype(jnp.int32).reshape(1)
    me = lax.axis_index("head").astype(jnp.int32).reshape(1)
    ids = jnp.concatenate([seq_index, me])
    rows, width = query.shape
    block_rows = rows * count
    heads = keys.shape[1] // HEAD_DIM
    picks = selected.shape[1]
    distances = range(1, picks)

    wanted = [shifted(selected, "seq", -d) for d in distances]
    pieces = split_queries(query, out_grad, me, heads)
    moved = [[p[0]] + [flipped(p[r], "head", r) for r in range(1, count)] for p in pieces]
    outgoing = gather_blocks(keys, values, wanted, seq_index, block_rows, heads)
    arrived = [
        [shifted(outgoing[head][d - 1], "seq", d) for d in distances] for head in range(heads)
    ]
    buffers = []
    shapes = [jax.ShapeDtypeStruct(query.shape, query.dtype)] * 2
    shapes += [jax.ShapeDtypeStruct(keys.shape, keys.dtype)] * 2
    results = []
    for head in range(heads):
        outs, grads, cleared = attend(
            me, selected, span_pos, moved[head], keys, values, arrived[head], head
        )
        buffers += cleared
        returned = [shifted(grads[d], "seq", -d) for d in distances]
        outs = [outs[0]] + [flipped(outs[r], "head", r) for r in range(1, count)]
        results.append((outs, [grads[0]] + returned + [grads[picks]]))
    for head in range(heads):
        outs, contributions = results[head]
        buffers = finish(
            ids, selected, span_pos, wanted, outs, contributions, buffers, shapes, head, heads
        )
    return tuple(buffers)


def solution(mesh):
    in_specs = (
        P(("seq", "head"), None),
        P("seq", "head"),
        P("seq", "head"),
        P(("seq", "head"), None),
        P("seq"),
        P("seq", None),
    )
    out_specs = (
        P(("seq", "head"), None),
        P(("seq", "head"), None),
        P("seq", "head"),
        P("seq", "head"),
    )
    return jax.shard_map(
        per_device, mesh=mesh, in_specs=in_specs, out_specs=out_specs, check_vma=False
    )
```

profile of v0, /device:TPU:6, one launch (start us, length us, event | category | flops | bytes accessed | tf_op | source)
XLA Modules:
  0.0 146.3 jit_solution(170728870202587606)
XLA Ops:
  3.9 2.0 %collective-permute-start = (s32[1,4]{1,0:T(1,128)}, s32[1,4]{1,0:T(1,128)S(1)}, u32[]{:S(2)}, u32[]{:S(2)}) collective-permute-start(s32[1,4]{1,0:T(1,128)} %chosen_ref.7), channel_id=1, source_target_pairs={{4,0},{8,4},{12,8},{16,12},{20,16},{24,20},{28,24},{5,1},{9,5},{13... | collective-permute-start | bytes 56 | tf_op jit(solution)/shard_map/ppermute | solution.py:25
  5.9 1.3 collective-permute-start.1
  7.2 1.3 collective-permute-start.2
  8.5 1.9 %collective-permute-done.refs_0_ = s32[1,4]{1,0:T(1,128)S(1)} collective-permute-done((s32[1,4]{1,0:T(1,128)}, s32[1,4]{1,0:T(1,128)S(1)}, u32[]{:S(2)}, u32[]{:S(2)}) %collective-permute-start) | collective-permute-done | bytes 48 | tf_op jit(solution)/shard_map/ppermute | solution.py:25
  12.0 3.7 %collective-permute-done.2.refs_2_ = s32[1,4]{1,0:T(1,128)S(1)} collective-permute-done((s32[1,4]{1,0:T(1,128)}, s32[1,4]{1,0:T(1,128)S(1)}, u32[]{:S(2)}, u32[]{:S(2)}) %collective-permute-start.2) | collective-permute-done | bytes 48 | tf_op jit(solution)/shard_map/ppermute | solution.py:25
  15.7 2.1 %gather_blocks.1 = (bf16[2,512,128]{2,1,0:T(8,128)(2,1)S(1)}, bf16[2,512,128]{2,1,0:T(8,128)(2,1)S(1)}, bf16[2,512,128]{2,1,0:T(8,128)(2,1)S(1)}, bf16[2,512,128...) custom-call(s32[1]{0:T(128)} %bitcast.seq_ref, ...), custom_call_target="tpu_custom_call" | custom-call | tf_op jit(solution)/shard_map/gather_blocks/pallas_call | solution.py:88
  17.8 3.4 %collective-permute-start.18 = (bf16[2,512,128]{2,1,0:T(8,128)(2,1)S(1)}, bf16[2,512,128]{2,1,0:T(8,128)(2,1)S(1)}, u32[]{:S(2)}, u32[]{:S(2)}) collective-permute-start(bf16[2,512,128]{2,1,0:T(8,128)(2,1)S(1)} %get-tuple-element.62), channel_id=1, source_target_pairs={{0,4},{4,8},{8,12},{12,16},{16,20},{20,24},{24,28},{1,5},{5,9},{9,... | collective-permute-start | bytes 786440 | tf_op jit(solution)/shard_map/ppermute | solution.py:25
  21.2 3.9 %collective-permute-start.19 = (bf16[2,512,128]{2,1,0:T(8,128)(2,1)S(1)}, bf16[2,512,128]{2,1,0:T(8,128)(2,1)S(1)}, u32[]{:S(2)}, u32[]{:S(2)}) collective-permute-start(bf16[2,512,128]{2,1,0:T(8,128)(2,1)S(1)} %get-tuple-element.63), channel_id=1, source_target_pairs={{0,8},{4,12},{8,16},{12,20},{16,24},{20,28},{1,9},{5,13},{9,17},{1... | collective-permute-start | bytes 786440 | tf_op jit(solution)/shard_map/ppermute | solution.py:25
  25.1 2.0 %collective-permute-start.20 = (bf16[2,512,128]{2,1,0:T(8,128)(2,1)S(1)}, bf16[2,512,128]{2,1,0:T(8,128)(2,1)S(1)}, u32[]{:S(2)}, u32[]{:S(2)}) collective-permute-start(bf16[2,512,128]{2,1,0:T(8,128)(2,1)S(1)} %get-tuple-element.64), channel_id=1, source_target_pairs={{0,12},{4,16},{8,20},{12,24},{16,28},{1,13},{5,17},{9,21},{13,25},... | collective-permute-start | bytes 786440 | tf_op jit(solution)/shard_map/ppermute | solution.py:25
  29.1 4.0 %collective-permute-start.6 = (bf16[2,512,128]{2,1,0:T(8,128)(2,1)S(1)}, bf16[2,512,128]{2,1,0:T(8,128)(2,1)S(1)}, u32[]{:S(2)}, u32[]{:S(2)}) collective-permute-start(bf16[2,512,128]{2,1,0:T(8,128)(2,1)S(1)} %get-tuple-element.46), channel_id=1, source_target_pairs={{0,4},{4,8},{8,12},{12,16},{16,20},{20,24},{24,28},{1,5},{5,9},{9,... | collective-permute-start | bytes 786440 | tf_op jit(solution)/shard_map/ppermute | solution.py:25
  33.4 9.5 %collective-permute-start.7 = (bf16[2,512,128]{2,1,0:T(8,128)(2,1)S(1)}, bf16[2,512,128]{2,1,0:T(8,128)(2,1)S(1)}, u32[]{:S(2)}, u32[]{:S(2)}) collective-permute-start(bf16[2,512,128]{2,1,0:T(8,128)(2,1)S(1)} %get-tuple-element.47), channel_id=1, source_target_pairs={{0,8},{4,12},{8,16},{12,20},{16,24},{20,28},{1,9},{5,13},{9,17},{1... | collective-permute-start | bytes 786440 | tf_op jit(solution)/shard_map/ppermute | solution.py:25
  42.9 2.4 %collective-permute-start.8 = (bf16[2,512,128]{2,1,0:T(8,128)(2,1)S(1)}, bf16[2,512,128]{2,1,0:T(8,128)(2,1)S(1)}, u32[]{:S(2)}, u32[]{:S(2)}) collective-permute-start(bf16[2,512,128]{2,1,0:T(8,128)(2,1)S(1)} %get-tuple-element.48), channel_id=1, source_target_pairs={{0,12},{4,16},{8,20},{12,24},{16,28},{1,13},{5,17},{9,21},{13,25},... | collective-permute-start | bytes 786440 | tf_op jit(solution)/shard_map/ppermute | solution.py:25
  45.3 23.1 %attend.3 = (bf16[2,128,512]{2,1,0:T(8,128)(2,1)S(1)}, bf16[2,128,512]{2,1,0:T(8,128)(2,1)S(1)}, bf16[2,128,512]{2,1,0:T(8,128)(2,1)S(1)}, bf16[2,128,512]{2,1,0...) custom-call(s32[1]{0:T(128)} %bitcast.1.me_ref, ...), custom_call_target="tpu_custom_call" | custom-call | flops 8053063680 | bytes 8388608 | tf_op jit(solution)/shard_map/attend/pallas_call | solution.py:213
  68.5 1.6 %collective-permute-start.22 = (bf16[2,128,512]{2,1,0:T(8,128)(2,1)S(1)}, bf16[2,128,512]{2,1,0:T(8,128)(2,1)S(1)}, u32[]{:S(2)}, u32[]{:S(2)}) collective-permute-start(bf16[2,128,512]{2,1,0:T(8,128)(2,1)S(1)} %get-tuple-element.67), channel_id=1, source_target_pairs={{0,2},{1,3},{2,0},{3,1},{4,6},{5,7},{6,4},{7,5},{8,10},{9,11},{10,... | collective-permute-start | bytes 786440 | tf_op jit(solution)/shard_map/ppermute | solution.py:30
  70.4 6.7 %collective-permute-start.24 = (bf16[2,512,128]{2,1,0:T(8,128)(2,1)S(1)}, bf16[2,512,128]{2,1,0:T(8,128)(2,1)S(1)}, u32[]{:S(2)}, u32[]{:S(2)}) collective-permute-start(bf16[2,512,128]{2,1,0:T(8,128)(2,1)S(1)} %get-tuple-element.70), channel_id=1, source_target_pairs={{4,0},{8,4},{12,8},{16,12},{20,16},{24,20},{28,24},{5,1},{9,5},{13... | collective-permute-start | bytes 786440 | tf_op jit(solution)/shard_map/ppermute | solution.py:25
  77.2 1.5 %collective-permute-start.25 = (bf16[2,512,128]{2,1,0:T(8,128)(2,1)S(1)}, bf16[2,512,128]{2,1,0:T(8,128)(2,1)S(1)}, u32[]{:S(2)}, u32[]{:S(2)}) collective-permute-start(bf16[2,512,128]{2,1,0:T(8,128)(2,1)S(1)} %get-tuple-element.71), channel_id=1, source_target_pairs={{8,0},{12,4},{16,8},{20,12},{24,16},{28,20},{9,1},{13,5},{17,9},{2... | collective-permute-start | bytes 786440 | tf_op jit(solution)/shard_map/ppermute | solution.py:25
  78.7 22.9 %attend.2 = (bf16[2,128,512]{2,1,0:T(8,128)(2,1)S(1)}, bf16[2,128,512]{2,1,0:T(8,128)(2,1)S(1)}, bf16[2,128,512]{2,1,0:T(8,128)(2,1)S(1)}, bf16[2,128,512]{2,1,0...) custom-call(s32[1]{0:T(128)} %bitcast.1.me_ref, ...), custom_call_target="tpu_custom_call" | custom-call | flops 8053063680 | bytes 8388608 | tf_op jit(solution)/shard_map/attend/pallas_call | solution.py:213
  102.9 1.6 %collective-permute-start.10 = (bf16[2,128,512]{2,1,0:T(8,128)(2,1)S(1)}, bf16[2,128,512]{2,1,0:T(8,128)(2,1)S(1)}, u32[]{:S(2)}, u32[]{:S(2)}) collective-permute-start(bf16[2,128,512]{2,1,0:T(8,128)(2,1)S(1)} %get-tuple-element.51), channel_id=1, source_target_pairs={{0,2},{1,3},{2,0},{3,1},{4,6},{5,7},{6,4},{7,5},{8,10},{9,11},{10,... | collective-permute-start | bytes 786440 | tf_op jit(solution)/shard_map/ppermute | solution.py:30
  104.5 1.9 %collective-permute-start.12 = (bf16[2,512,128]{2,1,0:T(8,128)(2,1)S(1)}, bf16[2,512,128]{2,1,0:T(8,128)(2,1)S(1)}, u32[]{:S(2)}, u32[]{:S(2)}) collective-permute-start(bf16[2,512,128]{2,1,0:T(8,128)(2,1)S(1)} %get-tuple-element.54), channel_id=1, source_target_pairs={{4,0},{8,4},{12,8},{16,12},{20,16},{24,20},{28,24},{5,1},{9,5},{13... | collective-permute-start | bytes 786440 | tf_op jit(solution)/shard_map/ppermute | solution.py:25
  106.5 1.3 collective-permute-start.13
  107.8 14.3 %collective-permute-done.26.refs_10_ = bf16[2,512,128]{2,1,0:T(8,128)(2,1)S(1)} collective-permute-done((bf16[2,512,128]{2,1,0:T(8,128)(2,1)S(1)}, bf16[2,512,128]{2,1,0:T(8,128)(2,1)S(1)}, u32[]{:S(2)}, u32[]{:S(2)}) %collective-permute-start.26) | collective-permute-done | bytes 262176 | tf_op jit(solution)/shard_map/ppermute | solution.py:25
  123.5 2.1 %finish.2 = (bf16[128,4096]{1,0:T(8,128)(2,1)}, bf16[128,4096]{1,0:T(8,128)(2,1)}, bf16[16384,256]{1,0:T(8,128)(2,1)}, bf16[16384,256]{1,0:T(8,128)(2,1)}) custom-call(s32[2]{0:T(128)S(1)} %pad_add_fusion.ids_ref, s32[1,4]{1,0:T(1,128)S(1)} %copy-done.2, s32[1]{0:T(128)S(6)} %copy.22.pos_ref, ...), custom_call_target="tpu_custom_call", output_to_operand_aliasing={{2}: (15, {}), {3}: (16, {})} | custom-call | tf_op jit(solution)/shard_map/finish/pallas_call | solution.py:329
  125.7 18.3 %collective-permute-done.14.refs_10_ = bf16[2,512,128]{2,1,0:T(8,128)(2,1)S(1)} collective-permute-done((bf16[2,512,128]{2,1,0:T(8,128)(2,1)S(1)}, bf16[2,512,128]{2,1,0:T(8,128)(2,1)S(1)}, u32[]{:S(2)}, u32[]{:S(2)}) %collective-permute-start.14) | collective-permute-done | bytes 262176 | tf_op jit(solution)/shard_map/ppermute | solution.py:25
  144.0 2.1 %finish.3 = (bf16[128,4096]{1,0:T(8,128)(2,1)}, bf16[128,4096]{1,0:T(8,128)(2,1)}, bf16[16384,256]{1,0:T(8,128)(2,1)}, bf16[16384,256]{1,0:T(8,128)(2,1)}) custom-call(s32[2]{0:T(128)S(1)} %pad_add_fusion.ids_ref, s32[1,4]{1,0:T(1,128)S(1)} %copy-done.2, ...), custom_call_target="tpu_custom_call", output_to_operand_aliasing={{0}: (15, {}), {1}: (16, {}), {2}: (17, {}), {3}: (18, {})} | custom-call | tf_op jit(solution)/shard_map/finish/pallas_call | solution.py:329
  (43 shorter events, 9.6 us)
Async XLA Ops:
  3.3 17.9 %collective-permute-start.15 = (bf16[2,128,512]{2,1,0:T(8,128)(2,1)S(1)}, bf16[2,128,512]{2,1,0:T(8,128)(2,1)S(1)}, u32[]{:S(2)}, u32[]{:S(2)}) collective-permute-start(bf16[2,128,512]{2,1,0:T(8,128)(2,1)S(1)} %get-tuple-element.59), channel_id=1, source_target_pairs={{0,1},{1,0},{2,3},{3,2},{4,5},{5,4},{6,7},{7,6},{8,9},{9,8},{10,11... | collective-permute-start | bytes 786440 | tf_op jit(solution)/shard_map/ppermute | solution.py:30
  3.3 21.8 %collective-permute-start.16 = (bf16[2,128,512]{2,1,0:T(8,128)(2,1)S(1)}, bf16[2,128,512]{2,1,0:T(8,128)(2,1)S(1)}, u32[]{:S(2)}, u32[]{:S(2)}) collective-permute-start(bf16[2,128,512]{2,1,0:T(8,128)(2,1)S(1)} %get-tuple-element.60), channel_id=1, source_target_pairs={{0,2},{1,3},{2,0},{3,1},{4,6},{5,7},{6,4},{7,5},{8,10},{9,11},{10,... | collective-permute-start | bytes 786440 | tf_op jit(solution)/shard_map/ppermute | solution.py:30
  10.4 17.4 %collective-permute-start.17 = (bf16[2,128,512]{2,1,0:T(8,128)(2,1)S(1)}, bf16[2,128,512]{2,1,0:T(8,128)(2,1)S(1)}, u32[]{:S(2)}, u32[]{:S(2)}) collective-permute-start(bf16[2,128,512]{2,1,0:T(8,128)(2,1)S(1)} %get-tuple-element.61), channel_id=1, source_target_pairs={{0,3},{1,2},{2,1},{3,0},{4,7},{5,6},{6,5},{7,4},{8,11},{9,10},{10,... | collective-permute-start | bytes 786440 | tf_op jit(solution)/shard_map/ppermute | solution.py:30
  11.5 17.6 %collective-permute-start.3 = (bf16[2,128,512]{2,1,0:T(8,128)(2,1)S(1)}, bf16[2,128,512]{2,1,0:T(8,128)(2,1)S(1)}, u32[]{:S(2)}, u32[]{:S(2)}) collective-permute-start(bf16[2,128,512]{2,1,0:T(8,128)(2,1)S(1)} %get-tuple-element.43), channel_id=1, source_target_pairs={{0,1},{1,0},{2,3},{3,2},{4,5},{5,4},{6,7},{7,6},{8,9},{9,8},{10,11... | collective-permute-start | bytes 786440 | tf_op jit(solution)/shard_map/ppermute | solution.py:30
  17.8 11.3 %collective-permute-start.18 = (bf16[2,512,128]{2,1,0:T(8,128)(2,1)S(1)}, bf16[2,512,128]{2,1,0:T(8,128)(2,1)S(1)}, u32[]{:S(2)}, u32[]{:S(2)}) collective-permute-start(bf16[2,512,128]{2,1,0:T(8,128)(2,1)S(1)} %get-tuple-element.62), channel_id=1, source_target_pairs={{0,4},{4,8},{8,12},{12,16},{16,20},{20,24},{24,28},{1,5},{5,9},{9,... | collective-permute-start | bytes 786440 | tf_op jit(solution)/shard_map/ppermute | solution.py:25
  21.2 12.3 %collective-permute-start.19 = (bf16[2,512,128]{2,1,0:T(8,128)(2,1)S(1)}, bf16[2,512,128]{2,1,0:T(8,128)(2,1)S(1)}, u32[]{:S(2)}, u32[]{:S(2)}) collective-permute-start(bf16[2,512,128]{2,1,0:T(8,128)(2,1)S(1)} %get-tuple-element.63), channel_id=1, source_target_pairs={{0,8},{4,12},{8,16},{12,20},{16,24},{20,28},{1,9},{5,13},{9,17},{1... | collective-permute-start | bytes 786440 | tf_op jit(solution)/shard_map/ppermute | solution.py:25
  25.1 17.8 %collective-permute-start.20 = (bf16[2,512,128]{2,1,0:T(8,128)(2,1)S(1)}, bf16[2,512,128]{2,1,0:T(8,128)(2,1)S(1)}, u32[]{:S(2)}, u32[]{:S(2)}) collective-permute-start(bf16[2,512,128]{2,1,0:T(8,128)(2,1)S(1)} %get-tuple-element.64), channel_id=1, source_target_pairs={{0,12},{4,16},{8,20},{12,24},{16,28},{1,13},{5,17},{9,21},{13,25},... | collective-permute-start | bytes 786440 | tf_op jit(solution)/shard_map/ppermute | solution.py:25
  27.8 40.7 %collective-permute-start.4 = (bf16[2,128,512]{2,1,0:T(8,128)(2,1)S(1)}, bf16[2,128,512]{2,1,0:T(8,128)(2,1)S(1)}, u32[]{:S(2)}, u32[]{:S(2)}) collective-permute-start(bf16[2,128,512]{2,1,0:T(8,128)(2,1)S(1)} %get-tuple-element.44), channel_id=1, source_target_pairs={{0,2},{1,3},{2,0},{3,1},{4,6},{5,7},{6,4},{7,5},{8,10},{9,11},{10,... | collective-permute-start | bytes 786440 | tf_op jit(solution)/shard_map/ppermute | solution.py:30
  29.1 39.5 %collective-permute-start.5 = (bf16[2,128,512]{2,1,0:T(8,128)(2,1)S(1)}, bf16[2,128,512]{2,1,0:T(8,128)(2,1)S(1)}, u32[]{:S(2)}, u32[]{:S(2)}) collective-permute-start(bf16[2,128,512]{2,1,0:T(8,128)(2,1)S(1)} %get-tuple-element.45), channel_id=1, source_target_pairs={{0,3},{1,2},{2,1},{3,0},{4,7},{5,6},{6,5},{7,4},{8,11},{9,10},{10,... | collective-permute-start | bytes 786440 | tf_op jit(solution)/shard_map/ppermute | solution.py:30
  29.1 41.1 %collective-permute-start.6 = (bf16[2,512,128]{2,1,0:T(8,128)(2,1)S(1)}, bf16[2,512,128]{2,1,0:T(8,128)(2,1)S(1)}, u32[]{:S(2)}, u32[]{:S(2)}) collective-permute-start(bf16[2,512,128]{2,1,0:T(8,128)(2,1)S(1)} %get-tuple-element.46), channel_id=1, source_target_pairs={{0,4},{4,8},{8,12},{12,16},{16,20},{20,24},{24,28},{1,5},{5,9},{9,... | collective-permute-start | bytes 786440 | tf_op jit(solution)/shard_map/ppermute | solution.py:25
  33.4 37.0 %collective-permute-start.7 = (bf16[2,512,128]{2,1,0:T(8,128)(2,1)S(1)}, bf16[2,512,128]{2,1,0:T(8,128)(2,1)S(1)}, u32[]{:S(2)}, u32[]{:S(2)}) collective-permute-start(bf16[2,512,128]{2,1,0:T(8,128)(2,1)S(1)} %get-tuple-element.47), channel_id=1, source_target_pairs={{0,8},{4,12},{8,16},{12,20},{16,24},{20,28},{1,9},{5,13},{9,17},{1... | collective-permute-start | bytes 786440 | tf_op jit(solution)/shard_map/ppermute | solution.py:25
  42.9 34.2 %collective-permute-start.8 = (bf16[2,512,128]{2,1,0:T(8,128)(2,1)S(1)}, bf16[2,512,128]{2,1,0:T(8,128)(2,1)S(1)}, u32[]{:S(2)}, u32[]{:S(2)}) collective-permute-start(bf16[2,512,128]{2,1,0:T(8,128)(2,1)S(1)} %get-tuple-element.48), channel_id=1, source_target_pairs={{0,12},{4,16},{8,20},{12,24},{16,28},{1,13},{5,17},{9,21},{13,25},... | collective-permute-start | bytes 786440 | tf_op jit(solution)/shard_map/ppermute | solution.py:25
  68.5 33.2 %collective-permute-start.21 = (bf16[2,128,512]{2,1,0:T(8,128)(2,1)S(1)}, bf16[2,128,512]{2,1,0:T(8,128)(2,1)S(1)}, u32[]{:S(2)}, u32[]{:S(2)}) collective-permute-start(bf16[2,128,512]{2,1,0:T(8,128)(2,1)S(1)} %get-tuple-element.66), channel_id=1, source_target_pairs={{0,1},{1,0},{2,3},{3,2},{4,5},{5,4},{6,7},{7,6},{8,9},{9,8},{10,11... | collective-permute-start | bytes 786440 | tf_op jit(solution)/shard_map/ppermute | solution.py:30
  68.5 34.4 %collective-permute-start.22 = (bf16[2,128,512]{2,1,0:T(8,128)(2,1)S(1)}, bf16[2,128,512]{2,1,0:T(8,128)(2,1)S(1)}, u32[]{:S(2)}, u32[]{:S(2)}) collective-permute-start(bf16[2,128,512]{2,1,0:T(8,128)(2,1)S(1)} %get-tuple-element.67), channel_id=1, source_target_pairs={{0,2},{1,3},{2,0},{3,1},{4,6},{5,7},{6,4},{7,5},{8,10},{9,11},{10,... | collective-permute-start | bytes 786440 | tf_op jit(solution)/shard_map/ppermute | solution.py:30
  70.1 34.4 %collective-permute-start.23 = (bf16[2,128,512]{2,1,0:T(8,128)(2,1)S(1)}, bf16[2,128,512]{2,1,0:T(8,128)(2,1)S(1)}, u32[]{:S(2)}, u32[]{:S(2)}) collective-permute-start(bf16[2,128,512]{2,1,0:T(8,128)(2,1)S(1)} %get-tuple-element.68), channel_id=1, source_target_pairs={{0,3},{1,2},{2,1},{3,0},{4,7},{5,6},{6,5},{7,4},{8,11},{9,10},{10,... | collective-permute-start | bytes 786440 | tf_op jit(solution)/shard_map/ppermute | solution.py:30
  70.4 34.1 %collective-permute-start.24 = (bf16[2,512,128]{2,1,0:T(8,128)(2,1)S(1)}, bf16[2,512,128]{2,1,0:T(8,128)(2,1)S(1)}, u32[]{:S(2)}, u32[]{:S(2)}) collective-permute-start(bf16[2,512,128]{2,1,0:T(8,128)(2,1)S(1)} %get-tuple-element.70), channel_id=1, source_target_pairs={{4,0},{8,4},{12,8},{16,12},{20,16},{24,20},{28,24},{5,1},{9,5},{13... | collective-permute-start | bytes 786440 | tf_op jit(solution)/shard_map/ppermute | solution.py:25
  77.2 29.3 %collective-permute-start.25 = (bf16[2,512,128]{2,1,0:T(8,128)(2,1)S(1)}, bf16[2,512,128]{2,1,0:T(8,128)(2,1)S(1)}, u32[]{:S(2)}, u32[]{:S(2)}) collective-permute-start(bf16[2,512,128]{2,1,0:T(8,128)(2,1)S(1)} %get-tuple-element.71), channel_id=1, source_target_pairs={{8,0},{12,4},{16,8},{20,12},{24,16},{28,20},{9,1},{13,5},{17,9},{2... | collective-permute-start | bytes 786440 | tf_op jit(solution)/shard_map/ppermute | solution.py:25
  101.6 20.5 %collective-permute-start.26 = (bf16[2,512,128]{2,1,0:T(8,128)(2,1)S(1)}, bf16[2,512,128]{2,1,0:T(8,128)(2,1)S(1)}, u32[]{:S(2)}, u32[]{:S(2)}) collective-permute-start(bf16[2,512,128]{2,1,0:T(8,128)(2,1)S(1)} %get-tuple-element.72), channel_id=1, source_target_pairs={{12,0},{16,4},{20,8},{24,12},{28,16},{13,1},{17,5},{21,9},{25,13},... | collective-permute-start | bytes 786440 | tf_op jit(solution)/shard_map/ppermute | solution.py:25
  102.9 20.4 %collective-permute-start.10 = (bf16[2,128,512]{2,1,0:T(8,128)(2,1)S(1)}, bf16[2,128,512]{2,1,0:T(8,128)(2,1)S(1)}, u32[]{:S(2)}, u32[]{:S(2)}) collective-permute-start(bf16[2,128,512]{2,1,0:T(8,128)(2,1)S(1)} %get-tuple-element.51), channel_id=1, source_target_pairs={{0,2},{1,3},{2,0},{3,1},{4,6},{5,7},{6,4},{7,5},{8,10},{9,11},{10,... | collective-permute-start | bytes 786440 | tf_op jit(solution)/shard_map/ppermute | solution.py:30
  104.5 21.2 %collective-permute-start.11 = (bf16[2,128,512]{2,1,0:T(8,128)(2,1)S(1)}, bf16[2,128,512]{2,1,0:T(8,128)(2,1)S(1)}, u32[]{:S(2)}, u32[]{:S(2)}) collective-permute-start(bf16[2,128,512]{2,1,0:T(8,128)(2,1)S(1)} %get-tuple-element.52), channel_id=1, source_target_pairs={{0,3},{1,2},{2,1},{3,0},{4,7},{5,6},{6,5},{7,4},{8,11},{9,10},{10,... | collective-permute-start | bytes 786440 | tf_op jit(solution)/shard_map/ppermute | solution.py:30
  104.5 21.2 %collective-permute-start.12 = (bf16[2,512,128]{2,1,0:T(8,128)(2,1)S(1)}, bf16[2,512,128]{2,1,0:T(8,128)(2,1)S(1)}, u32[]{:S(2)}, u32[]{:S(2)}) collective-permute-start(bf16[2,512,128]{2,1,0:T(8,128)(2,1)S(1)} %get-tuple-element.54), channel_id=1, source_target_pairs={{4,0},{8,4},{12,8},{16,12},{20,16},{24,20},{28,24},{5,1},{9,5},{13... | collective-permute-start | bytes 786440 | tf_op jit(solution)/shard_map/ppermute | solution.py:25
  106.5 19.2 %collective-permute-start.13 = (bf16[2,512,128]{2,1,0:T(8,128)(2,1)S(1)}, bf16[2,512,128]{2,1,0:T(8,128)(2,1)S(1)}, u32[]{:S(2)}, u32[]{:S(2)}) collective-permute-start(bf16[2,512,128]{2,1,0:T(8,128)(2,1)S(1)} %get-tuple-element.55), channel_id=1, source_target_pairs={{8,0},{12,4},{16,8},{20,12},{24,16},{28,20},{9,1},{13,5},{17,9},{2... | collective-permute-start | bytes 786440 | tf_op jit(solution)/shard_map/ppermute | solution.py:25
  122.1 21.9 %collective-permute-start.14 = (bf16[2,512,128]{2,1,0:T(8,128)(2,1)S(1)}, bf16[2,512,128]{2,1,0:T(8,128)(2,1)S(1)}, u32[]{:S(2)}, u32[]{:S(2)}) collective-permute-start(bf16[2,512,128]{2,1,0:T(8,128)(2,1)S(1)} %get-tuple-element.56), channel_id=1, source_target_pairs={{12,0},{16,4},{20,8},{24,12},{28,16},{13,1},{17,5},{21,9},{25,13},... | collective-permute-start | bytes 786440 | tf_op jit(solution)/shard_map/ppermute | solution.py:25
  123.4 20.6 %collective-permute-start.9 = (bf16[2,128,512]{2,1,0:T(8,128)(2,1)S(1)}, bf16[2,128,512]{2,1,0:T(8,128)(2,1)S(1)}, u32[]{:S(2)}, u32[]{:S(2)}) collective-permute-start(bf16[2,128,512]{2,1,0:T(8,128)(2,1)S(1)} %get-tuple-element.50), channel_id=1, source_target_pairs={{0,1},{1,0},{2,3},{3,2},{4,5},{5,4},{6,7},{7,6},{8,9},{9,8},{10,11... | collective-permute-start | bytes 786440 | tf_op jit(solution)/shard_map/ppermute | solution.py:30
  (6 other events, 52.7 us)
where the time goes:
time: 148 us; the launch traced here: 146 us
  Pallas kernels  52.6 us (36%)
  starting transfers between devices  49.9 us (34%)
  waiting for transfers between devices  39.5 us (27%)
  local copies, waits for them, and re-layouts  2.45 us (2%)
  between operations  1.78 us (1%)
    pallas_call x2, Pallas kernels, attend(): pl.pallas_call(kernel, grid_spec=pltpu.PrefetchScalarGridSpec(num_scalar_...  46.1 us
    ppermute x15, starting transfers between devices, shifted(): lax.ppermute(value, axis, [(source, source + steps) for source in range(f...  43.7 us
    ppermute x15, waiting for transfers between devices, shifted(): lax.ppermute(value, axis, [(source, source + steps) for source in range(f...  39.5 us
    ppermute x12, starting transfers between devices, flipped(): lax.ppermute(value, axis, [(source, source ^ mask) for source in range(co...  6.16 us
    pallas_call x2, Pallas kernels, finish(): pl.pallas_call(kernel, in_specs=[SMEM] * (3 + picks - 1) + [VMEM] * count...  4.25 us
  transfers between devices with their start and end apart: 27, of which 6 were waited for; matrix products, arithmetic and copies ran while one was open for 0% of the time, Pallas kernels for 34%

commit v1 on v0

v1 whole, which is shorter than its diff:
```python
import functools
import math

import jax
import jax.numpy as jnp
from jax import lax
from jax.experimental import pallas as pl
from jax.experimental.pallas import tpu as pltpu
from jax.sharding import PartitionSpec as P

HEAD_DIM = 128
MASKED = -1e30
VMEM_LIMIT = 63 << 20

ROWS_ROWS = (((1,), (1,)), ((), ()))
ROWS_COLS = (((1,), (0,)), ((), ()))
HBM = pl.BlockSpec(memory_space=pl.ANY)
SMEM = pl.BlockSpec(memory_space=pltpu.SMEM)
VMEM = pl.BlockSpec(memory_space=pltpu.VMEM)


def shifted(value, axis, steps):
    count = lax.axis_size(axis)
    first, last = (max(0, -steps), min(count, count - steps))
    return lax.ppermute(value, axis, [(source, source + steps) for source in range(first, last)])


def exchanged(value, axis):
    return lax.all_to_all(value, axis, split_axis=0, concat_axis=0, tiled=True)


def dot(left, right, dims):
    return lax.dot_general(left, right, dims, preferred_element_type=jnp.float32)


def prepare(query, out_grad, keys, values, wanted, seq_index, heads):
    rows, width = query.shape
    devices = lax.axis_size("head")
    part = width // (devices * heads)
    block = rows * devices
    shard_blocks = keys.shape[0] // block
    count = len(wanted)
    pairs = heads * count

    def kernel(seq_ref, *refs):
        entries = refs[:count]
        q_ref, g_ref, k_ref, v_ref, queries_ref = refs[count : count + 5]
        outs = refs[count + 5 : count + 5 + pairs]
        held, held_queries, in_sem, out_sem = refs[count + 5 + pairs :]
        reads, writes = [], []

        def through(source, middle, target):
            slot = len(reads)
            reads.append(pltpu.make_async_copy(source, middle, in_sem.at[slot]))
            writes.append(pltpu.make_async_copy(middle, target, out_sem.at[slot]))

        for head in range(heads):
            for d in range(count):
                local = entries[d][0, d + 1] - seq_ref[0] * shard_blocks
                local = jnp.clip(local, 0, shard_blocks - 1)
                place = pl.ds(pl.multiple_of(local * block, block), block)
                cols = pl.ds(head * HEAD_DIM, HEAD_DIM)
                pair = head * count + d
                for which, source in enumerate((k_ref, v_ref)):
                    through(source.at[place, cols], held.at[pair, which], outs[pair].at[which])
        for device in range(devices):
            for head in range(heads):
                cols = pl.ds((device * heads + head) * part, part)
                for which, source in enumerate((q_ref, g_ref)):
                    row = head * 2 + which
                    through(
                        source.at[:, cols],
                        held_queries.at[device, row],
                        queries_ref.at[device, row],
                    )
        for read in reads:
            read.start()
        for read, write in zip(reads, writes):
            read.wait()
            write.start()
        for write in writes:
            write.wait()

    copies = pairs * 2 + devices * heads * 2
    flat = pl.pallas_call(
        kernel,
        in_specs=[SMEM] * (1 + count) + [HBM] * 4,
        out_specs=[HBM] * (1 + pairs),
        out_shape=[jax.ShapeDtypeStruct((devices, heads * 2, rows, part), query.dtype)]
        + [jax.ShapeDtypeStruct((2, block, HEAD_DIM), keys.dtype)] * pairs,
        scratch_shapes=[
            pltpu.VMEM((pairs, 2, block, HEAD_DIM), keys.dtype),
            pltpu.VMEM((devices, heads * 2, rows, part), query.dtype),
            pltpu.SemaphoreType.DMA((copies,)),
            pltpu.SemaphoreType.DMA((copies,)),
        ],
        compiler_params=pltpu.CompilerParams(vmem_limit_bytes=VMEM_LIMIT),
        name="prepare",
    )(seq_index, *wanted, query, out_grad, keys, values)
    return flat[0], [flat[1 + head * count : 1 + (head + 1) * count] for head in range(heads)]


def attend(chosen, span_pos, queries, keys, values, arrived, outs, head):
    count, _, rows, part = queries.shape
    group = part // HEAD_DIM
    block = count * rows
    picks = chosen.shape[1]
    slots = picks + 1
    shard_blocks = keys.shape[0] // block
    scale = HEAD_DIM**-0.5
    log2e = math.log2(math.e)
    fresh = 2 if head == 0 else 0
    clear_rows = math.gcd(keys.shape[0], 2048)
    clear_steps = keys.shape[0] // clear_rows
    clear_scratch = []
    if fresh:
        clear_scratch.append(pltpu.VMEM((clear_rows, keys.shape[1]), keys.dtype))
        clear_scratch.append(pltpu.SemaphoreType.DMA((fresh * clear_steps,)))

    def kernel(chosen_ref, pos_ref, queries_ref, *refs):
        first_k, first_v, own_k, own_v = refs[:4]
        refs = refs[4:]
        arrived_refs, refs = refs[: picks - 1], refs[picks - 1 + len(outs) :]
        out_ref, refs = refs[0], refs[1:]
        grad_refs, refs = refs[:slots], refs[slots:]
        zero_refs, refs = refs[:fresh], refs[fresh:]
        s_ref, acc_k, acc_v, k_t, v_t = refs[:5]
        key_refs = [first_k] + [ref.at[0] for ref in arrived_refs] + [own_k]
        value_refs = [first_v] + [ref.at[1] for ref in arrived_refs] + [own_v]
        spans = [slice(slot * block, (slot + 1) * block) for slot in range(slots)]
        step = pl.program_id(0)
        clears = []
        if fresh:
            blank, blank_sem = refs[5:]
            for which, target in enumerate(zero_refs):
                for part in range(clear_steps):
                    place = target.at[pl.ds(part * clear_rows, clear_rows)]
                    slot = blank_sem.at[which * clear_steps + part]
                    clears.append(pltpu.make_async_copy(blank, place, slot))

        @pl.when(step == 0)
        def _():
            if fresh:
                blank[...] = jnp.zeros_like(blank)
            for clear in clears:
                clear.start()
            for slot in range(slots):
                k_t[:, spans[slot]] = key_refs[slot][...].T
                v_t[:, spans[slot]] = value_refs[slot][...].T

        q = queries_ref[:, 0].reshape(block, HEAD_DIM)
        g = queries_ref[:, 1].reshape(block, HEAD_DIM)
        top = jnp.full((1, block), MASKED, jnp.float32)
        for slot in range(slots):
            s = dot(key_refs[slot][...], q, ROWS_ROWS) * (scale * log2e)
            if slot == picks:
                key_pos = lax.broadcasted_iota(jnp.int32, (block, block), 0)
                query_pos = lax.broadcasted_iota(jnp.int32, (block, block), 1)
                s = jnp.where(key_pos <= query_pos, s, MASKED)
            else:
                s = jnp.where(chosen_ref[0, slot] >= 0, s, MASKED)
            s_ref[spans[slot]] = s
            top = jnp.maximum(top, jnp.max(s, axis=0, keepdims=True))
        total = jnp.zeros((1, block), jnp.float32)
        for slot in range(slots):
            e = jnp.exp2(s_ref[spans[slot]] - top)
            s_ref[spans[slot]] = e
            total = total + jnp.sum(e, axis=0, keepdims=True)
        inverse = 1.0 / total
        o_t = jnp.zeros((HEAD_DIM, block), jnp.float32)
        for slot in range(slots):
            w = s_ref[spans[slot]] * inverse
            s_ref[spans[slot]] = w
            low = w.astype(jnp.bfloat16)
            o_t = o_t + dot(v_t[:, spans[slot]], low, ROWS_COLS)
            before = jnp.where(step == 0, 0.0, acc_v[spans[slot]])
            acc_v[spans[slot]] = before + dot(low, g, ROWS_COLS)
        o_t = o_t.astype(jnp.bfloat16).astype(jnp.float32)
        delta = jnp.sum(g.T.astype(jnp.float32) * o_t, axis=0, keepdims=True)
        q_t = jnp.zeros((HEAD_DIM, block), jnp.float32)
        for slot in range(slots):
            w_grad = dot(value_refs[slot][...], g, ROWS_ROWS)
            s_grad = (s_ref[spans[slot]] * (w_grad - delta)).astype(jnp.bfloat16)
            q_t = q_t + dot(k_t[:, spans[slot]], s_grad, ROWS_COLS)
            before = jnp.where(step == 0, 0.0, acc_k[spans[slot]])
            acc_k[spans[slot]] = before + dot(s_grad, q, ROWS_COLS)
        o = o_t.T.astype(jnp.bfloat16)
        q_grad = (q_t * scale).T.astype(jnp.bfloat16)
        out_ref[:, 0] = o.reshape(count, rows, HEAD_DIM)
        out_ref[:, 1] = q_grad.reshape(count, rows, HEAD_DIM)

        @pl.when(step == group - 1)
        def _():
            for slot in range(slots):
                grad_refs[slot][0] = (acc_k[spans[slot]] * scale).astype(jnp.bfloat16)
                grad_refs[slot][1] = acc_v[spans[slot]].astype(jnp.bfloat16)
            for clear in clears:
                clear.wait()

    def first_index(step, chosen, pos):
        return (jnp.maximum(lax.rem(chosen[0, 0], shard_blocks), 0), head)

    def own_index(step, chosen, pos):
        return (pos[0], head)

    def whole_index(step, chosen, pos):
        return (0, 0, 0)

    piece = pl.BlockSpec((count, 2, rows, HEAD_DIM), lambda step, chosen, pos: (0, head, 0, step))
    pair = pl.BlockSpec((2, block, HEAD_DIM), whole_index)
    flops = 12 * block * slots * block * HEAD_DIM * group
    result = pl.pallas_call(
        kernel,
        grid_spec=pltpu.PrefetchScalarGridSpec(
            num_scalar_prefetch=2,
            grid=(group,),
            in_specs=[piece]
            + [pl.BlockSpec((block, HEAD_DIM), first_index)] * 2
            + [pl.BlockSpec((block, HEAD_DIM), own_index)] * 2
            + [pair] * (picks - 1)
            + [HBM] * len(outs),
            out_specs=[piece] + [pair] * slots + [HBM] * fresh,
            scratch_shapes=[
                pltpu.VMEM((slots * block, block), jnp.float32),
                pltpu.VMEM((slots * block, HEAD_DIM), jnp.float32),
                pltpu.VMEM((slots * block, HEAD_DIM), jnp.float32),
                pltpu.VMEM((HEAD_DIM, slots * block), jnp.bfloat16),
                pltpu.VMEM((HEAD_DIM, slots * block), jnp.bfloat16),
            ]
            + clear_scratch,
        ),
        out_shape=[jax.ShapeDtypeStruct(queries.shape, jnp.bfloat16)]
        + [jax.ShapeDtypeStruct((2, block, HEAD_DIM), jnp.bfloat16)] * slots
        + [jax.ShapeDtypeStruct(keys.shape, keys.dtype)] * fresh,
        compiler_params=pltpu.CompilerParams(vmem_limit_bytes=VMEM_LIMIT),
        cost_estimate=pl.CostEstimate(
            flops=flops, bytes_accessed=8 << 20, transcendentals=block * block * slots * group
        ),
        input_output_aliases={2 + 5 + picks - 1 + i: i for i in range(len(outs))},
        name="attend",
    )(chosen, span_pos, queries, keys, values, keys, values, *arrived, *outs)
    return (result[0], result[1 : 1 + slots], result[1 + slots :])


def finish(seq_index, chosen, span_pos, wanted, outs, contributions, buffers, shapes, head):
    slots = len(contributions)
    picks = slots - 1
    block = contributions[0].shape[1]
    shapes = shapes if outs else shapes[2:]

    def kernel(seq_ref, chosen_ref, pos_ref, *refs):
        wanted_refs, refs = refs[: picks - 1], refs[picks - 1 :]
        out_refs, refs = refs[: len(outs)], refs[len(outs) :]
        given, refs = refs[:slots], refs[slots:]
        refs = refs[len(buffers) :]
        row_refs, refs = refs[: len(shapes) - 2], refs[len(shapes) - 2 :]
        key_ref, value_ref, held, held_rows, sums, read_sem, row_sem, out_sem, grad_sem = refs
        seq = seq_ref[0]
        shard_blocks = key_ref.shape[0] // block
        copies, row_reads = [], []
        for out_ref in out_refs:
            devices, rows, _, part = out_ref.shape
            row_reads.append(pltpu.make_async_copy(out_ref, held_rows, row_sem))
            for place in range(devices * rows // 2):
                device, head_of = place // (rows // 2), place % (rows // 2)
                for which, target in enumerate(row_refs):
                    slot = place * 2 + which
                    piece = (device, head_of * 2 + which)
                    columns = target.at[:, pl.ds(place * part, part)]
                    middle = held_rows.at[piece]
                    copies.append(pltpu.make_async_copy(middle, columns, out_sem.at[slot]))
        reads = [
            pltpu.make_async_copy(given[i], held.at[i], read_sem.at[i]) for i in range(slots)
        ]
        for read in reads + row_reads:
            read.start()
        targets = [jnp.where(chosen_ref[0, 0] >= 0, chosen_ref[0, 0] - seq * shard_blocks, -1)]
        for d in range(1, picks):
            above = seq + d < lax.axis_size("seq")
            local = wanted_refs[d - 1][0, d] - seq * shard_blocks
            targets.append(jnp.where(above, local, -1))
        targets.append(pos_ref[0])
        present = [(t >= 0) & (t < shard_blocks) for t in targets]
        same = {}
        for i in range(slots):
            for j in range(i + 1, slots):
                same[i, j] = present[i] & (targets[i] == targets[j])

        def moves(i, source):
            start = pl.multiple_of(jnp.clip(targets[i], 0, shard_blocks - 1) * block, block)
            place = (pl.ds(start, block), pl.ds(head * HEAD_DIM, HEAD_DIM))
            return [
                pltpu.make_async_copy(source.at[which], target.at[place], grad_sem.at[i * 2 + which])
                for which, target in enumerate((key_ref, value_ref))
            ]

        leads = []
        for read in reads:
            read.wait()
        for i in range(slots):
            lead = present[i]
            for j in range(i):
                lead = lead & jnp.logical_not(same[j, i])
            shared = jnp.bool_(False)
            for j in range(i + 1, slots):
                shared = shared | same[i, j]
            leads.append(lead)

            @pl.when(lead & jnp.logical_not(shared))
            def _(i=i):
                for copy in moves(i, held.at[i]):
                    copy.start()

            @pl.when(lead & shared)
            def _(i=i):
                value = held[i].astype(jnp.float32)
                for j in range(i + 1, slots):
                    value = value + jnp.where(same[i, j], held[j].astype(jnp.float32), 0.0)
                sums[i] = value.astype(jnp.bfloat16)
                for copy in moves(i, sums.at[i]):
                    copy.start()

        for read in row_reads:
            read.wait()
        for copy in copies:
            copy.start()
        for i in range(slots):

            @pl.when(leads[i])
            def _(i=i):
                for copy in moves(i, held.at[i]):
                    copy.wait()

        for copy in copies:
            copy.wait()

    out_copies = outs[0].shape[0] * outs[0].shape[1] if outs else 1
    base = 3 + picks - 1 + len(outs) + slots
    return pl.pallas_call(
        kernel,
        in_specs=[SMEM] * (3 + picks - 1)
        + [HBM] * (len(outs) + slots + len(buffers)),
        out_specs=[HBM] * len(shapes),
        out_shape=shapes,
        scratch_shapes=[
            pltpu.VMEM((slots, 2, block, HEAD_DIM), jnp.bfloat16),
            pltpu.VMEM(outs[0].shape if outs else (16, HEAD_DIM), jnp.bfloat16),
            pltpu.VMEM((slots, 2, block, HEAD_DIM), jnp.bfloat16),
            pltpu.SemaphoreType.DMA((slots,)),
            pltpu.SemaphoreType.DMA,
            pltpu.SemaphoreType.DMA((out_copies,)),
            pltpu.SemaphoreType.DMA((slots * 2,)),
        ],
        input_output_aliases={base + i: len(shapes) - 2 + i for i in range(2)},
        compiler_params=pltpu.CompilerParams(vmem_limit_bytes=VMEM_LIMIT),
        name="finish",
    )(seq_index, chosen, span_pos, *wanted, *outs, *contributions, *buffers)


def per_device(query, keys, values, out_grad, span_pos, selected):
    seq_index = lax.axis_index("seq").astype(jnp.int32).reshape(1)
    heads = keys.shape[1] // HEAD_DIM
    distances = range(1, selected.shape[1])

    wanted = [shifted(selected, "seq", -d) for d in distances]
    queries, outgoing = prepare(query, out_grad, keys, values, wanted, seq_index, heads)
    queries = exchanged(queries, "head")
    arrived = [[shifted(piece[d - 1], "seq", d) for d in distances] for piece in outgoing]
    shapes = [jax.ShapeDtypeStruct(query.shape, query.dtype)] * 2
    shapes += [jax.ShapeDtypeStruct(keys.shape, keys.dtype)] * 2
    buffers, outs, results = [], [], []
    for head in range(heads):
        out, grads, cleared = attend(
            selected, span_pos, queries, keys, values, arrived[head], outs, head
        )
        buffers += cleared
        if results:
            out, grads, results[-1] = lax.optimization_barrier((out, grads, results[-1]))
        outs = [out]
        returned = [shifted(grads[d], "seq", -d) for d in distances]
        results.append([grads[0]] + returned + [grads[-1]])
    out = exchanged(outs[0], "head")
    for head in range(heads):
        given = [out] if head == heads - 1 else []
        buffers = finish(
            seq_index, selected, span_pos, wanted, given, results[head], buffers, shapes, head
        )
    return tuple(buffers)


def solution(mesh):
    in_specs = (
        P(("seq", "head"), None),
        P("seq", "head"),
        P("seq", "head"),
        P(("seq", "head"), None),
        P("seq"),
        P("seq", None),
    )
    out_specs = (
        P(("seq", "head"), None),
        P(("seq", "head"), None),
        P("seq", "head"),
        P("seq", "head"),
    )
    return jax.shard_map(
        per_device, mesh=mesh, in_specs=in_specs, out_specs=out_specs, check_vma=False
    )
```

time: 148 us -> 143 us (0.966)
  Pallas kernels: 52.6 us -> 60.3 us
  starting transfers between devices: 49.9 us -> 43.6 us
  waiting for transfers between devices: 39.5 us -> 35.3 us
    ppermute x15, starting transfers between devices: 43.7 us -> 33.5 us  [shifted(): lax.ppermute(value, axis, [(source, source + steps) for source in range(f...]
    all_to_all x0 -> x2, starting transfers between devices: none -> 10.1 us  [exchanged(): return lax.all_to_all(value, axis, split_axis=0, concat_axis=0, tiled=True)]
    ppermute x15, waiting for transfers between devices: 39.5 us -> 32.5 us  [shifted(): lax.ppermute(value, axis, [(source, source + steps) for source in range(f...]
    ppermute x12 -> x0, starting transfers between devices: 6.16 us -> none  [flipped(): lax.ppermute(value, axis, [(source, source ^ mask) for source in range(co...]
    pallas_call x4 -> x3, Pallas kernels: 6.51 us -> 12.2 us  [the longest x2 7.59 us: finish(): pl.pallas_call(kernel, in_specs=[SMEM] * (3 + picks - 1) + [HBM] * (len(o...]
    all_to_all x0 -> x2, waiting for transfers between devices: none -> 2.84 us  [exchanged(): return lax.all_to_all(value, axis, split_axis=0, concat_axis=0, tiled=True)]
    pallas_call x2, Pallas kernels: 46.1 us -> 48.1 us  [attend(): pl.pallas_call(kernel, grid_spec=pltpu.PrefetchScalarGridSpec(num_scalar_...]
  transfers between devices with their start and end apart: 27 -> 17, of which waited for: 6 -> 9; matrix products, arithmetic and copies ran while one was open for 0% -> 0% of each run, Pallas kernels for 34% -> 36%
where the time goes in v1:
time: 143 us; the launch traced here: 142 us
  Pallas kernels  60.3 us (42%)
  starting transfers between devices  43.6 us (30%)
  waiting for transfers between devices  35.3 us (25%)
  between operations  1.67 us (1%)
    pallas_call x2, Pallas kernels, attend(): pl.pallas_call(kernel, grid_spec=pltpu.PrefetchScalarGridSpec(num_scalar_...  48.1 us
    ppermute x15, starting transfers between devices, shifted(): lax.ppermute(value, axis, [(source, source + steps) for source in range(f...  33.5 us
    ppermute x15, waiting for transfers between devices, shifted(): lax.ppermute(value, axis, [(source, source + steps) for source in range(f...  32.5 us
    all_to_all x2, starting transfers between devices, exchanged(): return lax.all_to_all(value, axis, split_axis=0, concat_axis=0, tiled=True)  10.1 us
    pallas_call x2, Pallas kernels, finish(): pl.pallas_call(kernel, in_specs=[SMEM] * (3 + picks - 1) + [HBM] * (len(o...  7.59 us
    pallas_call x1, Pallas kernels, prepare(): pl.pallas_call(kernel, in_specs=[SMEM] * (1 + count) + [HBM] * 4, out_spe...  4.63 us
  transfers between devices with their start and end apart: 17, of which 9 were waited for; matrix products, arithmetic and copies ran while one was open for 0% of the time, Pallas kernels for 36%

profile of v1, /device:TPU:6, one launch (start us, length us, event | category | flops | bytes accessed | tf_op | source)
XLA Modules:
  0.0 142.1 jit_solution(1434105075321824178)
XLA Ops:
  3.2 2.4 %collective-permute-start = (s32[1,4]{1,0:T(1,128)}, s32[1,4]{1,0:T(1,128)S(1)}, u32[]{:S(2)}, u32[]{:S(2)}) collective-permute-start(s32[1,4]{1,0:T(1,128)} %chosen_ref.7), channel_id=1, source_target_pairs={{4,0},{8,4},{12,8},{16,12},{20,16},{24,20},{28,24},{5,1},{9,5},{13... | collective-permute-start | bytes 56 | tf_op jit(solution)/shard_map/ppermute | solution.py:25
  5.7 2.3 %collective-permute-done.2.refs_2_ = s32[1,4]{1,0:T(1,128)S(1)} collective-permute-done((s32[1,4]{1,0:T(1,128)}, s32[1,4]{1,0:T(1,128)S(1)}, u32[]{:S(2)}, u32[]{:S(2)}) %collective-permute-start.2) | collective-permute-done | bytes 48 | tf_op jit(solution)/shard_map/ppermute | solution.py:25
  8.1 1.6 %collective-permute-done.refs_0_ = s32[1,4]{1,0:T(1,128)S(1)} collective-permute-done((s32[1,4]{1,0:T(1,128)}, s32[1,4]{1,0:T(1,128)S(1)}, u32[]{:S(2)}, u32[]{:S(2)}) %collective-permute-start) | collective-permute-done | bytes 48 | tf_op jit(solution)/shard_map/ppermute | solution.py:25
  10.2 4.6 %prepare.1 = (bf16[4,4,128,512]{3,2,1,0:T(8,128)(2,1)}, bf16[2,512,128]{2,1,0:T(8,128)(2,1)}, bf16[2,512,128]{2,1,0:T(8,128)(2,1)}, bf16[2,512,128]{2,1,0:T(8,12...) custom-call(s32[1]{0:T(128)} %bitcast.seq_ref, ...), custom_call_target="tpu_custom_call" | custom-call | tf_op jit(solution)/shard_map/prepare/pallas_call | solution.py:85
  14.8 4.9 %all-to-all-start = ((bf16[4,4,128,512]{3,2,1,0:T(8,128)(2,1)}), bf16[4,4,128,512]{3,2,1,0:T(8,128)(2,1)}, u32[]{:S(2)}, u32[]{:S(2)}) async-start(bf16[4,4,128,512]{3,2,1,0:T(8,128)(2,1)} %get-tuple-element.38), calls=%async_computation | async-start | bytes 4194304 | tf_op jit(solution)/shard_map/all_to_all | solution.py:29
  19.8 3.3 %collective-permute-start.6 = (bf16[2,512,128]{2,1,0:T(8,128)(2,1)}, bf16[2,512,128]{2,1,0:T(8,128)(2,1)S(1)}, u32[]{:S(2)}, u32[]{:S(2)}) collective-permute-start(bf16[2,512,128]{2,1,0:T(8,128)(2,1)} %get-tuple-element.42), channel_id=1, source_target_pairs={{0,4},{4,8},{8,12},{12,16},{16,20},{20,24},{24,28},{1,5},{5,9},{9,... | collective-permute-start | bytes 786440 | tf_op jit(solution)/shard_map/ppermute | solution.py:25
  23.1 6.0 %collective-permute-start.7 = (bf16[2,512,128]{2,1,0:T(8,128)(2,1)}, bf16[2,512,128]{2,1,0:T(8,128)(2,1)}, u32[]{:S(2)}, u32[]{:S(2)}) collective-permute-start(bf16[2,512,128]{2,1,0:T(8,128)(2,1)} %get-tuple-element.43), channel_id=1, source_target_pairs={{0,8},{4,12},{8,16},{12,20},{16,24},{20,28},{1,9},{5,13},{9,17},{1... | collective-permute-start | bytes 786440 | tf_op jit(solution)/shard_map/ppermute | solution.py:25
  29.1 3.4 %collective-permute-start.8 = (bf16[2,512,128]{2,1,0:T(8,128)(2,1)}, bf16[2,512,128]{2,1,0:T(8,128)(2,1)}, u32[]{:S(2)}, u32[]{:S(2)}) collective-permute-start(bf16[2,512,128]{2,1,0:T(8,128)(2,1)} %get-tuple-element.44), channel_id=1, source_target_pairs={{0,12},{4,16},{8,20},{12,24},{16,28},{1,13},{5,17},{9,21},{13,25},... | collective-permute-start | bytes 786440 | tf_op jit(solution)/shard_map/ppermute | solution.py:25
  33.1 3.4 %collective-permute-start.3 = (bf16[2,512,128]{2,1,0:T(8,128)(2,1)}, bf16[2,512,128]{2,1,0:T(8,128)(2,1)S(1)}, u32[]{:S(2)}, u32[]{:S(2)}) collective-permute-start(bf16[2,512,128]{2,1,0:T(8,128)(2,1)} %get-tuple-element.39), channel_id=1, source_target_pairs={{0,4},{4,8},{8,12},{12,16},{16,20},{20,24},{24,28},{1,5},{5,9},{9,... | collective-permute-start | bytes 786440 | tf_op jit(solution)/shard_map/ppermute | solution.py:25
  36.5 1.3 collective-permute-start.4
  37.8 2.0 %collective-permute-start.5 = (bf16[2,512,128]{2,1,0:T(8,128)(2,1)}, bf16[2,512,128]{2,1,0:T(8,128)(2,1)}, u32[]{:S(2)}, u32[]{:S(2)}) collective-permute-start(bf16[2,512,128]{2,1,0:T(8,128)(2,1)} %get-tuple-element.41), channel_id=1, source_target_pairs={{0,12},{4,16},{8,20},{12,24},{16,28},{1,13},{5,17},{9,21},{13,25},... | collective-permute-start | bytes 786440 | tf_op jit(solution)/shard_map/ppermute | solution.py:25
  41.1 2.8 %all-to-all-done.queries_ref = bf16[4,4,128,512]{3,2,1,0:T(8,128)(2,1)} async-done(((bf16[4,4,128,512]{3,2,1,0:T(8,128)(2,1)}), bf16[4,4,128,512]{3,2,1,0:T(8,128)(2,1)}, u32[]{:S(2)}, u32[]{:S(2)}) %all-to-all-start) | async-done | bytes 2097184 | tf_op jit(solution)/shard_map/all_to_all | solution.py:29
  43.9 24.1 %attend.2 = (bf16[4,4,128,512]{3,2,1,0:T(8,128)(2,1)}, bf16[2,512,128]{2,1,0:T(8,128)(2,1)}, bf16[2,512,128]{2,1,0:T(8,128)(2,1)}, bf16[2,512,128]{2,1,0:T(8,128...) custom-call(s32[1,4]{1,0:T(1,128)} %chosen_ref.7, ...), custom_call_target="tpu_custom_call" | custom-call | flops 8053063680 | bytes 8388608 | tf_op jit(solution)/shard_map/attend/pallas_call | solution.py:212
  68.1 1.9 %collective-permute-start.9 = (bf16[2,512,128]{2,1,0:T(8,128)(2,1)}, bf16[2,512,128]{2,1,0:T(8,128)(2,1)S(1)}, u32[]{:S(2)}, u32[]{:S(2)}) collective-permute-start(bf16[2,512,128]{2,1,0:T(8,128)(2,1)} %get-tuple-element.53), channel_id=1, source_target_pairs={{4,0},{8,4},{12,8},{16,12},{20,16},{24,20},{28,24},{5,1},{9,5},{13... | collective-permute-start | bytes 786440 | tf_op jit(solution)/shard_map/ppermute | solution.py:25
  71.3 1.5 %collective-permute-start.11 = (bf16[2,512,128]{2,1,0:T(8,128)(2,1)}, bf16[2,512,128]{2,1,0:T(8,128)(2,1)}, u32[]{:S(2)}, u32[]{:S(2)}) collective-permute-start(bf16[2,512,128]{2,1,0:T(8,128)(2,1)} %get-tuple-element.55), channel_id=1, source_target_pairs={{12,0},{16,4},{20,8},{24,12},{28,16},{13,1},{17,5},{21,9},{25,13},... | collective-permute-start | bytes 786440 | tf_op jit(solution)/shard_map/ppermute | solution.py:25
  73.5 24.0 %attend.3 = (bf16[4,4,128,512]{3,2,1,0:T(8,128)(2,1)}, bf16[2,512,128]{2,1,0:T(8,128)(2,1)}, bf16[2,512,128]{2,1,0:T(8,128)(2,1)}, bf16[2,512,128]{2,1,0:T(8,128...) custom-call(s32[1,4]{1,0:T(1,128)} %chosen_ref.7, ...), custom_call_target="tpu_custom_call", output_to_operand_aliasing={{0}: (10, {})} | custom-call | flops 8053063680 | bytes 8388608 | tf_op jit(solution)/shard_map/attend/pallas_call | solution.py:212
  97.5 3.1 %collective-permute-done.11.refs_6_ = bf16[2,512,128]{2,1,0:T(8,128)(2,1)} collective-permute-done((bf16[2,512,128]{2,1,0:T(8,128)(2,1)}, bf16[2,512,128]{2,1,0:T(8,128)(2,1)}, u32[]{:S(2)}, u32[]{:S(2)}) %collective-permute-start.11) | collective-permute-done | bytes 262176 | tf_op jit(solution)/shard_map/ppermute | solution.py:25
  100.6 5.1 %all-to-all-start.1 = ((bf16[4,4,128,512]{3,2,1,0:T(8,128)(2,1)}), bf16[4,4,128,512]{3,2,1,0:T(8,128)(2,1)}, u32[]{:S(2)}, u32[]{:S(2)}) async-start(bf16[4,4,128,512]{3,2,1,0:T(8,128)(2,1)} %get-tuple-element.57), calls=%async_computation.1 | async-start | bytes 4194304 | tf_op jit(solution)/shard_map/all_to_all | solution.py:29
  105.7 1.9 %collective-permute-start.12 = (bf16[2,512,128]{2,1,0:T(8,128)(2,1)}, bf16[2,512,128]{2,1,0:T(8,128)(2,1)S(1)}, u32[]{:S(2)}, u32[]{:S(2)}) collective-permute-start(bf16[2,512,128]{2,1,0:T(8,128)(2,1)} %get-tuple-element.59), channel_id=1, source_target_pairs={{4,0},{8,4},{12,8},{16,12},{20,16},{24,20},{28,24},{5,1},{9,5},{13... | collective-permute-start | bytes 786440 | tf_op jit(solution)/shard_map/ppermute | solution.py:25
  110.2 3.3 %finish.2 = (bf16[16384,256]{1,0:T(8,128)(2,1)}, bf16[16384,256]{1,0:T(8,128)(2,1)}) custom-call(s32[1]{0:T(128)} %bitcast.seq_ref, s32[1,4]{1,0:T(1,128)} %chosen_ref.7, s32[1]{0:T(128)S(6)} %copy.20.pos_ref, s32[1,4]{1,0:T(1,128)} %copy-done.8, s32[1,4]{1,0:T(1,128)} %copy-done.7, ...), custom_call_target="tpu_custom_call", output_to_operand_aliasing={{0}: (11, {}), {1}: (12, {})} | custom-call | tf_op jit(solution)/shard_map/finish/pallas_call | solution.py:339
  113.5 4.3 %collective-permute-done.12.refs_5_ = bf16[2,512,128]{2,1,0:T(8,128)(2,1)S(1)} collective-permute-done((bf16[2,512,128]{2,1,0:T(8,128)(2,1)}, bf16[2,512,128]{2,1,0:T(8,128)(2,1)S(1)}, u32[]{:S(2)}, u32[]{:S(2)}) %collective-permute-start.12) | collective-permute-done | bytes 262176 | tf_op jit(solution)/shard_map/ppermute | solution.py:25
  117.8 2.9 %collective-permute-done.13.refs_6_ = bf16[2,512,128]{2,1,0:T(8,128)(2,1)S(1)} collective-permute-done((bf16[2,512,128]{2,1,0:T(8,128)(2,1)}, bf16[2,512,128]{2,1,0:T(8,128)(2,1)S(1)}, u32[]{:S(2)}, u32[]{:S(2)}) %collective-permute-start.13) | collective-permute-done | bytes 262176 | tf_op jit(solution)/shard_map/ppermute | solution.py:25
  120.8 16.9 %collective-permute-done.14.refs_7_ = bf16[2,512,128]{2,1,0:T(8,128)(2,1)} collective-permute-done((bf16[2,512,128]{2,1,0:T(8,128)(2,1)}, bf16[2,512,128]{2,1,0:T(8,128)(2,1)}, u32[]{:S(2)}, u32[]{:S(2)}) %collective-permute-start.14) | collective-permute-done | bytes 262176 | tf_op jit(solution)/shard_map/ppermute | solution.py:25
  137.6 4.3 %finish.3 = (bf16[128,4096]{1,0:T(8,128)(2,1)}, bf16[128,4096]{1,0:T(8,128)(2,1)}, bf16[16384,256]{1,0:T(8,128)(2,1)}, bf16[16384,256]{1,0:T(8,128)(2,1)}) custom-call(s32[1]{0:T(128)} %bitcast.seq_ref, s32[1,4]{1,0:T(1,128)} %chosen_ref.7, s32[1]{0:T(128)S(6)} %copy.20.pos_ref, s32[1,4]{1,0:T(1,128)} %copy-done.8, ...), custom_call_target="tpu_custom_call", output_to_operand_aliasing={{2}: (12, {}), {3}: (13, {})} | custom-call | tf_op jit(solution)/shard_map/finish/pallas_call | solution.py:339
  (33 shorter events, 9.1 us)
Async XLA Ops:
  0.6 7.4 %collective-permute-start.2 = (s32[1,4]{1,0:T(1,128)}, s32[1,4]{1,0:T(1,128)S(1)}, u32[]{:S(2)}, u32[]{:S(2)}) collective-permute-start(s32[1,4]{1,0:T(1,128)} %chosen_ref.7), channel_id=1, source_target_pairs={{12,0},{16,4},{20,8},{24,12},{28,16},{13,1},{17,5},{21,9},{25,13},... | collective-permute-start | bytes 56 | tf_op jit(solution)/shard_map/ppermute | solution.py:25
  1.9 6.2 %collective-permute-start.1 = (s32[1,4]{1,0:T(1,128)}, s32[1,4]{1,0:T(1,128)S(1)}, u32[]{:S(2)}, u32[]{:S(2)}) collective-permute-start(s32[1,4]{1,0:T(1,128)} %chosen_ref.7), channel_id=1, source_target_pairs={{8,0},{12,4},{16,8},{20,12},{24,16},{28,20},{9,1},{13,5},{17,9},{2... | collective-permute-start | bytes 56 | tf_op jit(solution)/shard_map/ppermute | solution.py:25
  3.2 6.5 %collective-permute-start = (s32[1,4]{1,0:T(1,128)}, s32[1,4]{1,0:T(1,128)S(1)}, u32[]{:S(2)}, u32[]{:S(2)}) collective-permute-start(s32[1,4]{1,0:T(1,128)} %chosen_ref.7), channel_id=1, source_target_pairs={{4,0},{8,4},{12,8},{16,12},{20,16},{24,20},{28,24},{5,1},{9,5},{13... | collective-permute-start | bytes 56 | tf_op jit(solution)/shard_map/ppermute | solution.py:25
  8.0 1.7 %copy-start.6 = (s32[1,4]{1,0:T(1,128)}, s32[1,4]{1,0:T(1,128)S(1)}, u32[]{:S(2)}) copy-start(s32[1,4]{1,0:T(1,128)S(1)} %collective-permute-done.2.refs_2_) | copy-start | bytes 52
  8.1 1.6 %copy-start.7 = (s32[1,4]{1,0:T(1,128)}, s32[1,4]{1,0:T(1,128)S(1)}, u32[]{:S(2)}) copy-start(s32[1,4]{1,0:T(1,128)S(1)} %collective-permute-done.1.refs_1_) | copy-start | bytes 52
  14.8 29.1 %all-to-all-start = ((bf16[4,4,128,512]{3,2,1,0:T(8,128)(2,1)}), bf16[4,4,128,512]{3,2,1,0:T(8,128)(2,1)}, u32[]{:S(2)}, u32[]{:S(2)}) async-start(bf16[4,4,128,512]{3,2,1,0:T(8,128)(2,1)} %get-tuple-element.38), calls=%async_computation | async-start | bytes 4194304 | tf_op jit(solution)/shard_map/all_to_all | solution.py:29
  19.8 18.0 %collective-permute-start.6 = (bf16[2,512,128]{2,1,0:T(8,128)(2,1)}, bf16[2,512,128]{2,1,0:T(8,128)(2,1)S(1)}, u32[]{:S(2)}, u32[]{:S(2)}) collective-permute-start(bf16[2,512,128]{2,1,0:T(8,128)(2,1)} %get-tuple-element.42), channel_id=1, source_target_pairs={{0,4},{4,8},{8,12},{12,16},{16,20},{20,24},{24,28},{1,5},{5,9},{9,... | collective-permute-start | bytes 786440 | tf_op jit(solution)/shard_map/ppermute | solution.py:25
  23.1 16.7 %collective-permute-start.7 = (bf16[2,512,128]{2,1,0:T(8,128)(2,1)}, bf16[2,512,128]{2,1,0:T(8,128)(2,1)}, u32[]{:S(2)}, u32[]{:S(2)}) collective-permute-start(bf16[2,512,128]{2,1,0:T(8,128)(2,1)} %get-tuple-element.43), channel_id=1, source_target_pairs={{0,8},{4,12},{8,16},{12,20},{16,24},{20,28},{1,9},{5,13},{9,17},{1... | collective-permute-start | bytes 786440 | tf_op jit(solution)/shard_map/ppermute | solution.py:25
  29.1 12.0 %collective-permute-start.8 = (bf16[2,512,128]{2,1,0:T(8,128)(2,1)}, bf16[2,512,128]{2,1,0:T(8,128)(2,1)}, u32[]{:S(2)}, u32[]{:S(2)}) collective-permute-start(bf16[2,512,128]{2,1,0:T(8,128)(2,1)} %get-tuple-element.44), channel_id=1, source_target_pairs={{0,12},{4,16},{8,20},{12,24},{16,28},{1,13},{5,17},{9,21},{13,25},... | collective-permute-start | bytes 786440 | tf_op jit(solution)/shard_map/ppermute | solution.py:25
  33.1 38.2 %collective-permute-start.3 = (bf16[2,512,128]{2,1,0:T(8,128)(2,1)}, bf16[2,512,128]{2,1,0:T(8,128)(2,1)S(1)}, u32[]{:S(2)}, u32[]{:S(2)}) collective-permute-start(bf16[2,512,128]{2,1,0:T(8,128)(2,1)} %get-tuple-element.39), channel_id=1, source_target_pairs={{0,4},{4,8},{8,12},{12,16},{16,20},{20,24},{24,28},{1,5},{5,9},{9,... | collective-permute-start | bytes 786440 | tf_op jit(solution)/shard_map/ppermute | solution.py:25
  36.5 36.3 %collective-permute-start.4 = (bf16[2,512,128]{2,1,0:T(8,128)(2,1)}, bf16[2,512,128]{2,1,0:T(8,128)(2,1)S(1)}, u32[]{:S(2)}, u32[]{:S(2)}) collective-permute-start(bf16[2,512,128]{2,1,0:T(8,128)(2,1)} %get-tuple-element.40), channel_id=1, source_target_pairs={{0,8},{4,12},{8,16},{12,20},{16,24},{20,28},{1,9},{5,13},{9,17},{1... | collective-permute-start | bytes 786440 | tf_op jit(solution)/shard_map/ppermute | solution.py:25
  37.8 6.2 %copy-start.4 = (bf16[2,512,128]{2,1,0:T(8,128)(2,1)}, bf16[2,512,128]{2,1,0:T(8,128)(2,1)S(1)}, u32[]{:S(2)}) copy-start(bf16[2,512,128]{2,1,0:T(8,128)(2,1)S(1)} %collective-permute-done.6.refs_4_) | copy-start | bytes 786436
  37.8 35.0 %collective-permute-start.5 = (bf16[2,512,128]{2,1,0:T(8,128)(2,1)}, bf16[2,512,128]{2,1,0:T(8,128)(2,1)}, u32[]{:S(2)}, u32[]{:S(2)}) collective-permute-start(bf16[2,512,128]{2,1,0:T(8,128)(2,1)} %get-tuple-element.41), channel_id=1, source_target_pairs={{0,12},{4,16},{8,20},{12,24},{16,28},{1,13},{5,17},{9,21},{13,25},... | collective-permute-start | bytes 786440 | tf_op jit(solution)/shard_map/ppermute | solution.py:25
  68.1 29.4 %collective-permute-start.9 = (bf16[2,512,128]{2,1,0:T(8,128)(2,1)}, bf16[2,512,128]{2,1,0:T(8,128)(2,1)S(1)}, u32[]{:S(2)}, u32[]{:S(2)}) collective-permute-start(bf16[2,512,128]{2,1,0:T(8,128)(2,1)} %get-tuple-element.53), channel_id=1, source_target_pairs={{4,0},{8,4},{12,8},{16,12},{20,16},{24,20},{28,24},{5,1},{9,5},{13... | collective-permute-start | bytes 786440 | tf_op jit(solution)/shard_map/ppermute | solution.py:25
  70.0 27.5 %collective-permute-start.10 = (bf16[2,512,128]{2,1,0:T(8,128)(2,1)}, bf16[2,512,128]{2,1,0:T(8,128)(2,1)}, u32[]{:S(2)}, u32[]{:S(2)}) collective-permute-start(bf16[2,512,128]{2,1,0:T(8,128)(2,1)} %get-tuple-element.54), channel_id=1, source_target_pairs={{8,0},{12,4},{16,8},{20,12},{24,16},{28,20},{9,1},{13,5},{17,9},{2... | collective-permute-start | bytes 786440 | tf_op jit(solution)/shard_map/ppermute | solution.py:25
  71.3 1.5 %copy-start = (bf16[2,512,128]{2,1,0:T(8,128)(2,1)}, bf16[2,512,128]{2,1,0:T(8,128)(2,1)S(1)}, u32[]{:S(2)}) copy-start(bf16[2,512,128]{2,1,0:T(8,128)(2,1)S(1)} %collective-permute-done.3.refs_4_) | copy-start | bytes 786436
  71.3 29.3 %collective-permute-start.11 = (bf16[2,512,128]{2,1,0:T(8,128)(2,1)}, bf16[2,512,128]{2,1,0:T(8,128)(2,1)}, u32[]{:S(2)}, u32[]{:S(2)}) collective-permute-start(bf16[2,512,128]{2,1,0:T(8,128)(2,1)} %get-tuple-element.55), channel_id=1, source_target_pairs={{12,0},{16,4},{20,8},{24,12},{28,16},{13,1},{17,5},{21,9},{25,13},... | collective-permute-start | bytes 786440 | tf_op jit(solution)/shard_map/ppermute | solution.py:25
  97.5 12.7 %copy-start.1 = (bf16[2,512,128]{2,1,0:T(8,128)(2,1)}, bf16[2,512,128]{2,1,0:T(8,128)(2,1)S(1)}, u32[]{:S(2)}) copy-start(bf16[2,512,128]{2,1,0:T(8,128)(2,1)S(1)} %collective-permute-done.9.refs_4_) | copy-start | bytes 786436
  100.6 37.1 %all-to-all-start.1 = ((bf16[4,4,128,512]{3,2,1,0:T(8,128)(2,1)}), bf16[4,4,128,512]{3,2,1,0:T(8,128)(2,1)}, u32[]{:S(2)}, u32[]{:S(2)}) async-start(bf16[4,4,128,512]{3,2,1,0:T(8,128)(2,1)} %get-tuple-element.57), calls=%async_computation.1 | async-start | bytes 4194304 | tf_op jit(solution)/shard_map/all_to_all | solution.py:29
  105.7 12.1 %collective-permute-start.12 = (bf16[2,512,128]{2,1,0:T(8,128)(2,1)}, bf16[2,512,128]{2,1,0:T(8,128)(2,1)S(1)}, u32[]{:S(2)}, u32[]{:S(2)}) collective-permute-start(bf16[2,512,128]{2,1,0:T(8,128)(2,1)} %get-tuple-element.59), channel_id=1, source_target_pairs={{4,0},{8,4},{12,8},{16,12},{20,16},{24,20},{28,24},{5,1},{9,5},{13... | collective-permute-start | bytes 786440 | tf_op jit(solution)/shard_map/ppermute | solution.py:25
  107.6 13.2 %collective-permute-start.13 = (bf16[2,512,128]{2,1,0:T(8,128)(2,1)}, bf16[2,512,128]{2,1,0:T(8,128)(2,1)S(1)}, u32[]{:S(2)}, u32[]{:S(2)}) collective-permute-start(bf16[2,512,128]{2,1,0:T(8,128)(2,1)} %get-tuple-element.60), channel_id=1, source_target_pairs={{8,0},{12,4},{16,8},{20,12},{24,16},{28,20},{9,1},{13,5},{17,9},{2... | collective-permute-start | bytes 786440 | tf_op jit(solution)/shard_map/ppermute | solution.py:25
  108.9 28.7 %collective-permute-start.14 = (bf16[2,512,128]{2,1,0:T(8,128)(2,1)}, bf16[2,512,128]{2,1,0:T(8,128)(2,1)}, u32[]{:S(2)}, u32[]{:S(2)}) collective-permute-start(bf16[2,512,128]{2,1,0:T(8,128)(2,1)} %get-tuple-element.61), channel_id=1, source_target_pairs={{12,0},{16,4},{20,8},{24,12},{28,16},{13,1},{17,5},{21,9},{25,13},... | collective-permute-start | bytes 786440 | tf_op jit(solution)/shard_map/ppermute | solution.py:25
  117.8 19.8 %copy-start.3 = (bf16[2,512,128]{2,1,0:T(8,128)(2,1)}, bf16[2,512,128]{2,1,0:T(8,128)(2,1)S(1)}, u32[]{:S(2)}) copy-start(bf16[2,512,128]{2,1,0:T(8,128)(2,1)S(1)} %collective-permute-done.12.refs_5_) | copy-start | bytes 786436
  120.8 16.9 %copy-start.5 = (bf16[2,512,128]{2,1,0:T(8,128)(2,1)}, bf16[2,512,128]{2,1,0:T(8,128)(2,1)S(1)}, u32[]{:S(2)}) copy-start(bf16[2,512,128]{2,1,0:T(8,128)(2,1)S(1)} %collective-permute-done.13.refs_6_) | copy-start | bytes 786436
  (2 other events, 1.2 us)

commit v2 on v1

--- a/solution.py
+++ b/solution.py
@@ -109,6 +109,7 @@
     shard_blocks = keys.shape[0] // block
     scale = HEAD_DIM**-0.5
     log2e = math.log2(math.e)
+    parts = [range((slots + 1) // 2), range((slots + 1) // 2, slots)]
     fresh = 2 if head == 0 else 0
     clear_rows = math.gcd(keys.shape[0], 2048)
     clear_steps = keys.shape[0] // clear_rows
@@ -124,14 +125,14 @@
         out_ref, refs = refs[0], refs[1:]
         grad_refs, refs = refs[:slots], refs[slots:]
         zero_refs, refs = refs[:fresh], refs[fresh:]
-        s_ref, acc_k, acc_v, k_t, v_t = refs[:5]
+        s_ref, acc_k, acc_v, k_t, v_t, k_all, v_all = refs[:7]
         key_refs = [first_k] + [ref.at[0] for ref in arrived_refs] + [own_k]
         value_refs = [first_v] + [ref.at[1] for ref in arrived_refs] + [own_v]
         spans = [slice(slot * block, (slot + 1) * block) for slot in range(slots)]
         step = pl.program_id(0)
         clears = []
         if fresh:
-            blank, blank_sem = refs[5:]
+            blank, blank_sem = refs[7:]
             for which, target in enumerate(zero_refs):
                 for part in range(clear_steps):
                     place = target.at[pl.ds(part * clear_rows, clear_rows)]
@@ -144,46 +145,56 @@
                 blank[...] = jnp.zeros_like(blank)
             for clear in clears:
                 clear.start()
+            acc_k[...] = jnp.zeros_like(acc_k)
+            acc_v[...] = jnp.zeros_like(acc_v)
             for slot in range(slots):
+                k_all[spans[slot]] = key_refs[slot][...]
+                v_all[spans[slot]] = value_refs[slot][...]
                 k_t[:, spans[slot]] = key_refs[slot][...].T
                 v_t[:, spans[slot]] = value_refs[slot][...].T
 
         q = queries_ref[:, 0].reshape(block, HEAD_DIM)
         g = queries_ref[:, 1].reshape(block, HEAD_DIM)
         top = jnp.full((1, block), MASKED, jnp.float32)
-        for slot in range(slots):
-            s = dot(key_refs[slot][...], q, ROWS_ROWS) * (scale * log2e)
-            if slot == picks:
-                key_pos = lax.broadcasted_iota(jnp.int32, (block, block), 0)
-                query_pos = lax.broadcasted_iota(jnp.int32, (block, block), 1)
-                s = jnp.where(key_pos <= query_pos, s, MASKED)
-            else:
-                s = jnp.where(chosen_ref[0, slot] >= 0, s, MASKED)
-            s_ref[spans[slot]] = s
-            top = jnp.maximum(top, jnp.max(s, axis=0, keepdims=True))
+        for part_slots in parts:
+            start = part_slots[0] * block
+            rows_of = slice(start, (part_slots[-1] + 1) * block)
+            scores = dot(k_all[rows_of], q, ROWS_ROWS) * (scale * log2e)
+            for slot in part_slots:
+                s = scores[slot * block - start : (slot + 1) * block - start]
+                if slot == picks:
+                    key_pos = lax.broadcasted_iota(jnp.int32, (block, block), 0)
+                    query_pos = lax.broadcasted_iota(jnp.int32, (block, block), 1)
+                    s = jnp.where(key_pos <= query_pos, s, MASKED)
+                s_ref[spans[slot]] = s
+                slot_top = jnp.max(s, axis=0, keepdims=True)
+                if slot < picks:
+                    slot_top = jnp.where(chosen_ref[0, slot] >= 0, slot_top, MASKED)
+                top = jnp.maximum(top, slot_top)
         total = jnp.zeros((1, block), jnp.float32)
         for slot in range(slots):
-            e = jnp.exp2(s_ref[spans[slot]] - top)
+            level = top if slot == picks else jnp.where(chosen_ref[0, slot] >= 0, top, -MASKED)
+            e = jnp.exp2(s_ref[spans[slot]] - level)
             s_ref[spans[slot]] = e
             total = total + jnp.sum(e, axis=0, keepdims=True)
         inverse = 1.0 / total
         o_t = jnp.zeros((HEAD_DIM, block), jnp.float32)
-        for slot in range(slots):
-            w = s_ref[spans[slot]] * inverse
-            s_ref[spans[slot]] = w
+        for part_slots in parts:
+            rows_of = slice(part_slots[0] * block, (part_slots[-1] + 1) * block)
+            w = s_ref[rows_of] * inverse
+            s_ref[rows_of] = w
             low = w.astype(jnp.bfloat16)
-            o_t = o_t + dot(v_t[:, spans[slot]], low, ROWS_COLS)
-            before = jnp.where(step == 0, 0.0, acc_v[spans[slot]])
-            acc_v[spans[slot]] = before + dot(low, g, ROWS_COLS)
+            o_t = o_t + dot(v_t[:, rows_of], low, ROWS_COLS)
+            acc_v[rows_of] += dot(low, g, ROWS_COLS)
         o_t = o_t.astype(jnp.bfloat16).astype(jnp.float32)
         delta = jnp.sum(g.T.astype(jnp.float32) * o_t, axis=0, keepdims=True)
         q_t = jnp.zeros((HEAD_DIM, block), jnp.float32)
-        for slot in range(slots):
-            w_grad = dot(value_refs[slot][...], g, ROWS_ROWS)
-            s_grad = (s_ref[spans[slot]] * (w_grad - delta)).astype(jnp.bfloat16)
-            q_t = q_t + dot(k_t[:, spans[slot]], s_grad, ROWS_COLS)
-            before = jnp.where(step == 0, 0.0, acc_k[spans[slot]])
-            acc_k[spans[slot]] = before + dot(s_grad, q, ROWS_COLS)
+        for part_slots in parts:
+            rows_of = slice(part_slots[0] * block, (part_slots[-1] + 1) * block)
+            w_grad = dot(v_all[rows_of], g, ROWS_ROWS)
+            s_grad = (s_ref[rows_of] * (w_grad - delta)).astype(jnp.bfloat16)
+            q_t = q_t + dot(k_t[:, rows_of], s_grad, ROWS_COLS)
+            acc_k[rows_of] += dot(s_grad, q, ROWS_COLS)
         o = o_t.T.astype(jnp.bfloat16)
         q_grad = (q_t * scale).T.astype(jnp.bfloat16)
         out_ref[:, 0] = o.reshape(count, rows, HEAD_DIM)
@@ -226,6 +237,8 @@
                 pltpu.VMEM((slots * block, HEAD_DIM), jnp.float32),
                 pltpu.VMEM((HEAD_DIM, slots * block), jnp.bfloat16),
                 pltpu.VMEM((HEAD_DIM, slots * block), jnp.bfloat16),
+                pltpu.VMEM((slots * block, HEAD_DIM), jnp.bfloat16),
+                pltpu.VMEM((slots * block, HEAD_DIM), jnp.bfloat16),
             ]
             + clear_scratch,
         ),

time: 143 us -> 140 us (0.979)
  Pallas kernels: 60.3 us -> 57.1 us
    pallas_call x2, Pallas kernels: 48.1 us -> 45.1 us  [attend(): pl.pallas_call(kernel, grid_spec=pltpu.PrefetchScalarGridSpec(num_scalar_...]
  transfers between devices with their start and end apart: 17 -> 17, of which waited for: 9 -> 9; matrix products, arithmetic and copies ran while one was open for 0% -> 0% of each run, Pallas kernels for 36% -> 35%
where the time goes in v2:
time: 140 us; the launch traced here: 139 us
  Pallas kernels  57.1 us (41%)
  starting transfers between devices  43.6 us (31%)
  waiting for transfers between devices  35.6 us (25%)
  between operations  1.67 us (1%)
    pallas_call x2, Pallas kernels, attend(): pl.pallas_call(kernel, grid_spec=pltpu.PrefetchScalarGridSpec(num_scalar_...  45.1 us
    ppermute x15, starting transfers between devices, shifted(): lax.ppermute(value, axis, [(source, source + steps) for source in range(f...  33.5 us
    ppermute x15, waiting for transfers between devices, shifted(): lax.ppermute(value, axis, [(source, source + steps) for source in range(f...  32.7 us
    all_to_all x2, starting transfers between devices, exchanged(): return lax.all_to_all(value, axis, split_axis=0, concat_axis=0, tiled=True)  10.1 us
    pallas_call x2, Pallas kernels, finish(): pl.pallas_call(kernel, in_specs=[SMEM] * (3 + picks - 1) + [HBM] * (len(o...  7.35 us
    pallas_call x1, Pallas kernels, prepare(): pl.pallas_call(kernel, in_specs=[SMEM] * (1 + count) + [HBM] * 4, out_spe...  4.63 us
    all_to_all x2, waiting for transfers between devices, exchanged(): return lax.all_to_all(value, axis, split_axis=0, concat_axis=0, tiled=True)  2.84 us
  transfers between devices with their start and end apart: 17, of which 9 were waited for; matrix products, arithmetic and copies ran while one was open for 0% of the time, Pallas kernels for 35%

profile of v2, /device:TPU:6, one launch (start us, length us, event | category | flops | bytes accessed | tf_op | source)
XLA Modules:
  0.0 139.1 jit_solution(8522658751829643487)
XLA Ops:
  3.2 2.4 %collective-permute-start = (s32[1,4]{1,0:T(1,128)}, s32[1,4]{1,0:T(1,128)S(1)}, u32[]{:S(2)}, u32[]{:S(2)}) collective-permute-start(s32[1,4]{1,0:T(1,128)} %chosen_ref.7), channel_id=1, source_target_pairs={{4,0},{8,4},{12,8},{16,12},{20,16},{24,20},{28,24},{5,1},{9,5},{13... | collective-permute-start | bytes 56 | tf_op jit(solution)/shard_map/ppermute | solution.py:25
  5.7 2.3 %collective-permute-done.2.refs_2_ = s32[1,4]{1,0:T(1,128)S(1)} collective-permute-done((s32[1,4]{1,0:T(1,128)}, s32[1,4]{1,0:T(1,128)S(1)}, u32[]{:S(2)}, u32[]{:S(2)}) %collective-permute-start.2) | collective-permute-done | bytes 48 | tf_op jit(solution)/shard_map/ppermute | solution.py:25
  8.1 1.6 %collective-permute-done.refs_0_ = s32[1,4]{1,0:T(1,128)S(1)} collective-permute-done((s32[1,4]{1,0:T(1,128)}, s32[1,4]{1,0:T(1,128)S(1)}, u32[]{:S(2)}, u32[]{:S(2)}) %collective-permute-start) | collective-permute-done | bytes 48 | tf_op jit(solution)/shard_map/ppermute | solution.py:25
  10.2 4.6 %prepare.1 = (bf16[4,4,128,512]{3,2,1,0:T(8,128)(2,1)}, bf16[2,512,128]{2,1,0:T(8,128)(2,1)}, bf16[2,512,128]{2,1,0:T(8,128)(2,1)}, bf16[2,512,128]{2,1,0:T(8,12...) custom-call(s32[1]{0:T(128)} %bitcast.seq_ref, ...), custom_call_target="tpu_custom_call" | custom-call | tf_op jit(solution)/shard_map/prepare/pallas_call | solution.py:85
  14.8 4.9 %all-to-all-start = ((bf16[4,4,128,512]{3,2,1,0:T(8,128)(2,1)}), bf16[4,4,128,512]{3,2,1,0:T(8,128)(2,1)}, u32[]{:S(2)}, u32[]{:S(2)}) async-start(bf16[4,4,128,512]{3,2,1,0:T(8,128)(2,1)} %get-tuple-element.38), calls=%async_computation | async-start | bytes 4194304 | tf_op jit(solution)/shard_map/all_to_all | solution.py:29
  19.8 3.3 %collective-permute-start.6 = (bf16[2,512,128]{2,1,0:T(8,128)(2,1)}, bf16[2,512,128]{2,1,0:T(8,128)(2,1)S(1)}, u32[]{:S(2)}, u32[]{:S(2)}) collective-permute-start(bf16[2,512,128]{2,1,0:T(8,128)(2,1)} %get-tuple-element.42), channel_id=1, source_target_pairs={{0,4},{4,8},{8,12},{12,16},{16,20},{20,24},{24,28},{1,5},{5,9},{9,... | collective-permute-start | bytes 786440 | tf_op jit(solution)/shard_map/ppermute | solution.py:25
  23.1 6.0 %collective-permute-start.7 = (bf16[2,512,128]{2,1,0:T(8,128)(2,1)}, bf16[2,512,128]{2,1,0:T(8,128)(2,1)}, u32[]{:S(2)}, u32[]{:S(2)}) collective-permute-start(bf16[2,512,128]{2,1,0:T(8,128)(2,1)} %get-tuple-element.43), channel_id=1, source_target_pairs={{0,8},{4,12},{8,16},{12,20},{16,24},{20,28},{1,9},{5,13},{9,17},{1... | collective-permute-start | bytes 786440 | tf_op jit(solution)/shard_map/ppermute | solution.py:25
  29.1 3.4 %collective-permute-start.8 = (bf16[2,512,128]{2,1,0:T(8,128)(2,1)}, bf16[2,512,128]{2,1,0:T(8,128)(2,1)}, u32[]{:S(2)}, u32[]{:S(2)}) collective-permute-start(bf16[2,512,128]{2,1,0:T(8,128)(2,1)} %get-tuple-element.44), channel_id=1, source_target_pairs={{0,12},{4,16},{8,20},{12,24},{16,28},{1,13},{5,17},{9,21},{13,25},... | collective-permute-start | bytes 786440 | tf_op jit(solution)/shard_map/ppermute | solution.py:25
  33.1 3.4 %collective-permute-start.3 = (bf16[2,512,128]{2,1,0:T(8,128)(2,1)}, bf16[2,512,128]{2,1,0:T(8,128)(2,1)S(1)}, u32[]{:S(2)}, u32[]{:S(2)}) collective-permute-start(bf16[2,512,128]{2,1,0:T(8,128)(2,1)} %get-tuple-element.39), channel_id=1, source_target_pairs={{0,4},{4,8},{8,12},{12,16},{16,20},{20,24},{24,28},{1,5},{5,9},{9,... | collective-permute-start | bytes 786440 | tf_op jit(solution)/shard_map/ppermute | solution.py:25
  36.5 1.3 collective-permute-start.4
  37.8 2.0 %collective-permute-start.5 = (bf16[2,512,128]{2,1,0:T(8,128)(2,1)}, bf16[2,512,128]{2,1,0:T(8,128)(2,1)}, u32[]{:S(2)}, u32[]{:S(2)}) collective-permute-start(bf16[2,512,128]{2,1,0:T(8,128)(2,1)} %get-tuple-element.41), channel_id=1, source_target_pairs={{0,12},{4,16},{8,20},{12,24},{16,28},{1,13},{5,17},{9,21},{13,25},... | collective-permute-start | bytes 786440 | tf_op jit(solution)/shard_map/ppermute | solution.py:25
  41.1 2.8 %all-to-all-done.queries_ref = bf16[4,4,128,512]{3,2,1,0:T(8,128)(2,1)} async-done(((bf16[4,4,128,512]{3,2,1,0:T(8,128)(2,1)}), bf16[4,4,128,512]{3,2,1,0:T(8,128)(2,1)}, u32[]{:S(2)}, u32[]{:S(2)}) %all-to-all-start) | async-done | bytes 2097184 | tf_op jit(solution)/shard_map/all_to_all | solution.py:29
  43.9 22.6 %attend.2 = (bf16[4,4,128,512]{3,2,1,0:T(8,128)(2,1)}, bf16[2,512,128]{2,1,0:T(8,128)(2,1)}, bf16[2,512,128]{2,1,0:T(8,128)(2,1)}, bf16[2,512,128]{2,1,0:T(8,128...) custom-call(s32[1,4]{1,0:T(1,128)} %chosen_ref.7, ...), custom_call_target="tpu_custom_call" | custom-call | flops 8053063680 | bytes 8388608 | tf_op jit(solution)/shard_map/attend/pallas_call | solution.py:223
  66.6 1.9 %collective-permute-start.9 = (bf16[2,512,128]{2,1,0:T(8,128)(2,1)}, bf16[2,512,128]{2,1,0:T(8,128)(2,1)S(1)}, u32[]{:S(2)}, u32[]{:S(2)}) collective-permute-start(bf16[2,512,128]{2,1,0:T(8,128)(2,1)} %get-tuple-element.53), channel_id=1, source_target_pairs={{4,0},{8,4},{12,8},{16,12},{20,16},{24,20},{28,24},{5,1},{9,5},{13... | collective-permute-start | bytes 786440 | tf_op jit(solution)/shard_map/ppermute | solution.py:25
  69.8 1.5 %collective-permute-start.11 = (bf16[2,512,128]{2,1,0:T(8,128)(2,1)}, bf16[2,512,128]{2,1,0:T(8,128)(2,1)}, u32[]{:S(2)}, u32[]{:S(2)}) collective-permute-start(bf16[2,512,128]{2,1,0:T(8,128)(2,1)} %get-tuple-element.55), channel_id=1, source_target_pairs={{12,0},{16,4},{20,8},{24,12},{28,16},{13,1},{17,5},{21,9},{25,13},... | collective-permute-start | bytes 786440 | tf_op jit(solution)/shard_map/ppermute | solution.py:25
  72.0 22.5 %attend.3 = (bf16[4,4,128,512]{3,2,1,0:T(8,128)(2,1)}, bf16[2,512,128]{2,1,0:T(8,128)(2,1)}, bf16[2,512,128]{2,1,0:T(8,128)(2,1)}, bf16[2,512,128]{2,1,0:T(8,128...) custom-call(s32[1,4]{1,0:T(1,128)} %chosen_ref.7, ...), custom_call_target="tpu_custom_call", output_to_operand_aliasing={{0}: (10, {})} | custom-call | flops 8053063680 | bytes 8388608 | tf_op jit(solution)/shard_map/attend/pallas_call | solution.py:223
  94.5 4.6 %collective-permute-done.11.refs_6_ = bf16[2,512,128]{2,1,0:T(8,128)(2,1)} collective-permute-done((bf16[2,512,128]{2,1,0:T(8,128)(2,1)}, bf16[2,512,128]{2,1,0:T(8,128)(2,1)}, u32[]{:S(2)}, u32[]{:S(2)}) %collective-permute-start.11) | collective-permute-done | bytes 262176 | tf_op jit(solution)/shard_map/ppermute | solution.py:25
  99.1 5.1 %all-to-all-start.1 = ((bf16[4,4,128,512]{3,2,1,0:T(8,128)(2,1)}), bf16[4,4,128,512]{3,2,1,0:T(8,128)(2,1)}, u32[]{:S(2)}, u32[]{:S(2)}) async-start(bf16[4,4,128,512]{3,2,1,0:T(8,128)(2,1)} %get-tuple-element.57), calls=%async_computation.1 | async-start | bytes 4194304 | tf_op jit(solution)/shard_map/all_to_all | solution.py:29
  104.2 1.9 %collective-permute-start.12 = (bf16[2,512,128]{2,1,0:T(8,128)(2,1)}, bf16[2,512,128]{2,1,0:T(8,128)(2,1)S(1)}, u32[]{:S(2)}, u32[]{:S(2)}) collective-permute-start(bf16[2,512,128]{2,1,0:T(8,128)(2,1)} %get-tuple-element.59), channel_id=1, source_target_pairs={{4,0},{8,4},{12,8},{16,12},{20,16},{24,20},{28,24},{5,1},{9,5},{13... | collective-permute-start | bytes 786440 | tf_op jit(solution)/shard_map/ppermute | solution.py:25
  108.7 3.1 %finish.2 = (bf16[16384,256]{1,0:T(8,128)(2,1)}, bf16[16384,256]{1,0:T(8,128)(2,1)}) custom-call(s32[1]{0:T(128)} %bitcast.seq_ref, s32[1,4]{1,0:T(1,128)} %chosen_ref.7, s32[1]{0:T(128)S(6)} %copy.20.pos_ref, s32[1,4]{1,0:T(1,128)} %copy-done.8, s32[1,4]{1,0:T(1,128)} %copy-done.7, ...), custom_call_target="tpu_custom_call", output_to_operand_aliasing={{0}: (11, {}), {1}: (12, {})} | custom-call | tf_op jit(solution)/shard_map/finish/pallas_call | solution.py:352
  111.8 4.5 %collective-permute-done.12.refs_5_ = bf16[2,512,128]{2,1,0:T(8,128)(2,1)S(1)} collective-permute-done((bf16[2,512,128]{2,1,0:T(8,128)(2,1)}, bf16[2,512,128]{2,1,0:T(8,128)(2,1)S(1)}, u32[]{:S(2)}, u32[]{:S(2)}) %collective-permute-start.12) | collective-permute-done | bytes 262176 | tf_op jit(solution)/shard_map/ppermute | solution.py:25
  116.4 1.4 %collective-permute-done.13.refs_6_ = bf16[2,512,128]{2,1,0:T(8,128)(2,1)S(1)} collective-permute-done((bf16[2,512,128]{2,1,0:T(8,128)(2,1)}, bf16[2,512,128]{2,1,0:T(8,128)(2,1)S(1)}, u32[]{:S(2)}, u32[]{:S(2)}) %collective-permute-start.13) | collective-permute-done | bytes 262176 | tf_op jit(solution)/shard_map/ppermute | solution.py:25
  117.8 16.9 %collective-permute-done.14.refs_7_ = bf16[2,512,128]{2,1,0:T(8,128)(2,1)} collective-permute-done((bf16[2,512,128]{2,1,0:T(8,128)(2,1)}, bf16[2,512,128]{2,1,0:T(8,128)(2,1)}, u32[]{:S(2)}, u32[]{:S(2)}) %collective-permute-start.14) | collective-permute-done | bytes 262176 | tf_op jit(solution)/shard_map/ppermute | solution.py:25
  134.7 4.3 %finish.3 = (bf16[128,4096]{1,0:T(8,128)(2,1)}, bf16[128,4096]{1,0:T(8,128)(2,1)}, bf16[16384,256]{1,0:T(8,128)(2,1)}, bf16[16384,256]{1,0:T(8,128)(2,1)}) custom-call(s32[1]{0:T(128)} %bitcast.seq_ref, s32[1,4]{1,0:T(1,128)} %chosen_ref.7, s32[1]{0:T(128)S(6)} %copy.20.pos_ref, s32[1,4]{1,0:T(1,128)} %copy-done.8, ...), custom_call_target="tpu_custom_call", output_to_operand_aliasing={{2}: (12, {}), {3}: (13, {})} | custom-call | tf_op jit(solution)/shard_map/finish/pallas_call | solution.py:352
  (33 shorter events, 9.1 us)
Async XLA Ops:
  0.6 7.4 %collective-permute-start.2 = (s32[1,4]{1,0:T(1,128)}, s32[1,4]{1,0:T(1,128)S(1)}, u32[]{:S(2)}, u32[]{:S(2)}) collective-permute-start(s32[1,4]{1,0:T(1,128)} %chosen_ref.7), channel_id=1, source_target_pairs={{12,0},{16,4},{20,8},{24,12},{28,16},{13,1},{17,5},{21,9},{25,13},... | collective-permute-start | bytes 56 | tf_op jit(solution)/shard_map/ppermute | solution.py:25
  1.9 6.2 %collective-permute-start.1 = (s32[1,4]{1,0:T(1,128)}, s32[1,4]{1,0:T(1,128)S(1)}, u32[]{:S(2)}, u32[]{:S(2)}) collective-permute-start(s32[1,4]{1,0:T(1,128)} %chosen_ref.7), channel_id=1, source_target_pairs={{8,0},{12,4},{16,8},{20,12},{24,16},{28,20},{9,1},{13,5},{17,9},{2... | collective-permute-start | bytes 56 | tf_op jit(solution)/shard_map/ppermute | solution.py:25
  3.2 6.5 %collective-permute-start = (s32[1,4]{1,0:T(1,128)}, s32[1,4]{1,0:T(1,128)S(1)}, u32[]{:S(2)}, u32[]{:S(2)}) collective-permute-start(s32[1,4]{1,0:T(1,128)} %chosen_ref.7), channel_id=1, source_target_pairs={{4,0},{8,4},{12,8},{16,12},{20,16},{24,20},{28,24},{5,1},{9,5},{13... | collective-permute-start | bytes 56 | tf_op jit(solution)/shard_map/ppermute | solution.py:25
  8.0 1.7 %copy-start.6 = (s32[1,4]{1,0:T(1,128)}, s32[1,4]{1,0:T(1,128)S(1)}, u32[]{:S(2)}) copy-start(s32[1,4]{1,0:T(1,128)S(1)} %collective-permute-done.2.refs_2_) | copy-start | bytes 52
  8.1 1.6 %copy-start.7 = (s32[1,4]{1,0:T(1,128)}, s32[1,4]{1,0:T(1,128)S(1)}, u32[]{:S(2)}) copy-start(s32[1,4]{1,0:T(1,128)S(1)} %collective-permute-done.1.refs_1_) | copy-start | bytes 52
  14.8 29.1 %all-to-all-start = ((bf16[4,4,128,512]{3,2,1,0:T(8,128)(2,1)}), bf16[4,4,128,512]{3,2,1,0:T(8,128)(2,1)}, u32[]{:S(2)}, u32[]{:S(2)}) async-start(bf16[4,4,128,512]{3,2,1,0:T(8,128)(2,1)} %get-tuple-element.38), calls=%async_computation | async-start | bytes 4194304 | tf_op jit(solution)/shard_map/all_to_all | solution.py:29
  19.8 18.0 %collective-permute-start.6 = (bf16[2,512,128]{2,1,0:T(8,128)(2,1)}, bf16[2,512,128]{2,1,0:T(8,128)(2,1)S(1)}, u32[]{:S(2)}, u32[]{:S(2)}) collective-permute-start(bf16[2,512,128]{2,1,0:T(8,128)(2,1)} %get-tuple-element.42), channel_id=1, source_target_pairs={{0,4},{4,8},{8,12},{12,16},{16,20},{20,24},{24,28},{1,5},{5,9},{9,... | collective-permute-start | bytes 786440 | tf_op jit(solution)/shard_map/ppermute | solution.py:25
  23.1 16.7 %collective-permute-start.7 = (bf16[2,512,128]{2,1,0:T(8,128)(2,1)}, bf16[2,512,128]{2,1,0:T(8,128)(2,1)}, u32[]{:S(2)}, u32[]{:S(2)}) collective-permute-start(bf16[2,512,128]{2,1,0:T(8,128)(2,1)} %get-tuple-element.43), channel_id=1, source_target_pairs={{0,8},{4,12},{8,16},{12,20},{16,24},{20,28},{1,9},{5,13},{9,17},{1... | collective-permute-start | bytes 786440 | tf_op jit(solution)/shard_map/ppermute | solution.py:25
  29.1 12.0 %collective-permute-start.8 = (bf16[2,512,128]{2,1,0:T(8,128)(2,1)}, bf16[2,512,128]{2,1,0:T(8,128)(2,1)}, u32[]{:S(2)}, u32[]{:S(2)}) collective-permute-start(bf16[2,512,128]{2,1,0:T(8,128)(2,1)} %get-tuple-element.44), channel_id=1, source_target_pairs={{0,12},{4,16},{8,20},{12,24},{16,28},{1,13},{5,17},{9,21},{13,25},... | collective-permute-start | bytes 786440 | tf_op jit(solution)/shard_map/ppermute | solution.py:25
  33.1 36.7 %collective-permute-start.3 = (bf16[2,512,128]{2,1,0:T(8,128)(2,1)}, bf16[2,512,128]{2,1,0:T(8,128)(2,1)S(1)}, u32[]{:S(2)}, u32[]{:S(2)}) collective-permute-start(bf16[2,512,128]{2,1,0:T(8,128)(2,1)} %get-tuple-element.39), channel_id=1, source_target_pairs={{0,4},{4,8},{8,12},{12,16},{16,20},{20,24},{24,28},{1,5},{5,9},{9,... | collective-permute-start | bytes 786440 | tf_op jit(solution)/shard_map/ppermute | solution.py:25
  36.5 34.9 %collective-permute-start.4 = (bf16[2,512,128]{2,1,0:T(8,128)(2,1)}, bf16[2,512,128]{2,1,0:T(8,128)(2,1)S(1)}, u32[]{:S(2)}, u32[]{:S(2)}) collective-permute-start(bf16[2,512,128]{2,1,0:T(8,128)(2,1)} %get-tuple-element.40), channel_id=1, source_target_pairs={{0,8},{4,12},{8,16},{12,20},{16,24},{20,28},{1,9},{5,13},{9,17},{1... | collective-permute-start | bytes 786440 | tf_op jit(solution)/shard_map/ppermute | solution.py:25
  37.8 6.2 %copy-start.4 = (bf16[2,512,128]{2,1,0:T(8,128)(2,1)}, bf16[2,512,128]{2,1,0:T(8,128)(2,1)S(1)}, u32[]{:S(2)}) copy-start(bf16[2,512,128]{2,1,0:T(8,128)(2,1)S(1)} %collective-permute-done.6.refs_4_) | copy-start | bytes 786436
  37.8 33.6 %collective-permute-start.5 = (bf16[2,512,128]{2,1,0:T(8,128)(2,1)}, bf16[2,512,128]{2,1,0:T(8,128)(2,1)}, u32[]{:S(2)}, u32[]{:S(2)}) collective-permute-start(bf16[2,512,128]{2,1,0:T(8,128)(2,1)} %get-tuple-element.41), channel_id=1, source_target_pairs={{0,12},{4,16},{8,20},{12,24},{16,28},{1,13},{5,17},{9,21},{13,25},... | collective-permute-start | bytes 786440 | tf_op jit(solution)/shard_map/ppermute | solution.py:25
  66.6 27.9 %collective-permute-start.9 = (bf16[2,512,128]{2,1,0:T(8,128)(2,1)}, bf16[2,512,128]{2,1,0:T(8,128)(2,1)S(1)}, u32[]{:S(2)}, u32[]{:S(2)}) collective-permute-start(bf16[2,512,128]{2,1,0:T(8,128)(2,1)} %get-tuple-element.53), channel_id=1, source_target_pairs={{4,0},{8,4},{12,8},{16,12},{20,16},{24,20},{28,24},{5,1},{9,5},{13... | collective-permute-start | bytes 786440 | tf_op jit(solution)/shard_map/ppermute | solution.py:25
  68.5 26.0 %collective-permute-start.10 = (bf16[2,512,128]{2,1,0:T(8,128)(2,1)}, bf16[2,512,128]{2,1,0:T(8,128)(2,1)}, u32[]{:S(2)}, u32[]{:S(2)}) collective-permute-start(bf16[2,512,128]{2,1,0:T(8,128)(2,1)} %get-tuple-element.54), channel_id=1, source_target_pairs={{8,0},{12,4},{16,8},{20,12},{24,16},{28,20},{9,1},{13,5},{17,9},{2... | collective-permute-start | bytes 786440 | tf_op jit(solution)/shard_map/ppermute | solution.py:25
  69.8 1.5 %copy-start = (bf16[2,512,128]{2,1,0:T(8,128)(2,1)}, bf16[2,512,128]{2,1,0:T(8,128)(2,1)S(1)}, u32[]{:S(2)}) copy-start(bf16[2,512,128]{2,1,0:T(8,128)(2,1)S(1)} %collective-permute-done.3.refs_4_) | copy-start | bytes 786436
  69.8 29.3 %collective-permute-start.11 = (bf16[2,512,128]{2,1,0:T(8,128)(2,1)}, bf16[2,512,128]{2,1,0:T(8,128)(2,1)}, u32[]{:S(2)}, u32[]{:S(2)}) collective-permute-start(bf16[2,512,128]{2,1,0:T(8,128)(2,1)} %get-tuple-element.55), channel_id=1, source_target_pairs={{12,0},{16,4},{20,8},{24,12},{28,16},{13,1},{17,5},{21,9},{25,13},... | collective-permute-start | bytes 786440 | tf_op jit(solution)/shard_map/ppermute | solution.py:25
  94.5 14.2 %copy-start.1 = (bf16[2,512,128]{2,1,0:T(8,128)(2,1)}, bf16[2,512,128]{2,1,0:T(8,128)(2,1)S(1)}, u32[]{:S(2)}) copy-start(bf16[2,512,128]{2,1,0:T(8,128)(2,1)S(1)} %collective-permute-done.9.refs_4_) | copy-start | bytes 786436
  99.1 35.6 %all-to-all-start.1 = ((bf16[4,4,128,512]{3,2,1,0:T(8,128)(2,1)}), bf16[4,4,128,512]{3,2,1,0:T(8,128)(2,1)}, u32[]{:S(2)}, u32[]{:S(2)}) async-start(bf16[4,4,128,512]{3,2,1,0:T(8,128)(2,1)} %get-tuple-element.57), calls=%async_computation.1 | async-start | bytes 4194304 | tf_op jit(solution)/shard_map/all_to_all | solution.py:29
  104.2 12.1 %collective-permute-start.12 = (bf16[2,512,128]{2,1,0:T(8,128)(2,1)}, bf16[2,512,128]{2,1,0:T(8,128)(2,1)S(1)}, u32[]{:S(2)}, u32[]{:S(2)}) collective-permute-start(bf16[2,512,128]{2,1,0:T(8,128)(2,1)} %get-tuple-element.59), channel_id=1, source_target_pairs={{4,0},{8,4},{12,8},{16,12},{20,16},{24,20},{28,24},{5,1},{9,5},{13... | collective-permute-start | bytes 786440 | tf_op jit(solution)/shard_map/ppermute | solution.py:25
  106.1 11.6 %collective-permute-start.13 = (bf16[2,512,128]{2,1,0:T(8,128)(2,1)}, bf16[2,512,128]{2,1,0:T(8,128)(2,1)S(1)}, u32[]{:S(2)}, u32[]{:S(2)}) collective-permute-start(bf16[2,512,128]{2,1,0:T(8,128)(2,1)} %get-tuple-element.60), channel_id=1, source_target_pairs={{8,0},{12,4},{16,8},{20,12},{24,16},{28,20},{9,1},{13,5},{17,9},{2... | collective-permute-start | bytes 786440 | tf_op jit(solution)/shard_map/ppermute | solution.py:25
  107.4 27.2 %collective-permute-start.14 = (bf16[2,512,128]{2,1,0:T(8,128)(2,1)}, bf16[2,512,128]{2,1,0:T(8,128)(2,1)}, u32[]{:S(2)}, u32[]{:S(2)}) collective-permute-start(bf16[2,512,128]{2,1,0:T(8,128)(2,1)} %get-tuple-element.61), channel_id=1, source_target_pairs={{12,0},{16,4},{20,8},{24,12},{28,16},{13,1},{17,5},{21,9},{25,13},... | collective-permute-start | bytes 786440 | tf_op jit(solution)/shard_map/ppermute | solution.py:25
  116.4 18.3 %copy-start.3 = (bf16[2,512,128]{2,1,0:T(8,128)(2,1)}, bf16[2,512,128]{2,1,0:T(8,128)(2,1)S(1)}, u32[]{:S(2)}) copy-start(bf16[2,512,128]{2,1,0:T(8,128)(2,1)S(1)} %collective-permute-done.12.refs_5_) | copy-start | bytes 786436
  117.8 16.9 %copy-start.5 = (bf16[2,512,128]{2,1,0:T(8,128)(2,1)}, bf16[2,512,128]{2,1,0:T(8,128)(2,1)S(1)}, u32[]{:S(2)}) copy-start(bf16[2,512,128]{2,1,0:T(8,128)(2,1)S(1)} %collective-permute-done.13.refs_6_) | copy-start | bytes 786436
  (2 other events, 1.2 us)

commit v3 on v2

--- a/solution.py
+++ b/solution.py
@@ -49,37 +49,40 @@
         held, held_queries, in_sem, out_sem = refs[count + 5 + pairs :]
         reads, writes = [], []
 
-        def through(source, middle, target):
-            slot = len(reads)
-            reads.append(pltpu.make_async_copy(source, middle, in_sem.at[slot]))
-            writes.append(pltpu.make_async_copy(middle, target, out_sem.at[slot]))
-
-        for head in range(heads):
-            for d in range(count):
-                local = entries[d][0, d + 1] - seq_ref[0] * shard_blocks
-                local = jnp.clip(local, 0, shard_blocks - 1)
-                place = pl.ds(pl.multiple_of(local * block, block), block)
-                cols = pl.ds(head * HEAD_DIM, HEAD_DIM)
-                pair = head * count + d
-                for which, source in enumerate((k_ref, v_ref)):
-                    through(source.at[place, cols], held.at[pair, which], outs[pair].at[which])
-        for device in range(devices):
-            for head in range(heads):
-                cols = pl.ds((device * heads + head) * part, part)
-                for which, source in enumerate((q_ref, g_ref)):
-                    row = head * 2 + which
-                    through(
-                        source.at[:, cols],
-                        held_queries.at[device, row],
-                        queries_ref.at[device, row],
+        def read(source, middle):
+            reads.append(pltpu.make_async_copy(source, middle, in_sem.at[len(reads)]))
+            writes.append([])
+
+        def write(middle, target):
+            slot = out_sem.at[sum(map(len, writes))]
+            writes[-1].append(pltpu.make_async_copy(middle, target, slot))
+
+        for d in range(count):
+            local = entries[d][0, d + 1] - seq_ref[0] * shard_blocks
+            local = jnp.clip(local, 0, shard_blocks - 1)
+            place = pl.ds(pl.multiple_of(local * block, block), block)
+            for which, source in enumerate((k_ref, v_ref)):
+                read(source.at[place], held.at[d, which])
+                for head in range(heads):
+                    cols = pl.ds(head * HEAD_DIM, HEAD_DIM)
+                    write(held.at[d, which, :, cols], outs[head * count + d].at[which])
+        for which, source in enumerate((q_ref, g_ref)):
+            read(source, held_queries.at[which])
+            for device in range(devices):
+                for head in range(heads):
+                    cols = pl.ds((device * heads + head) * part, part)
+                    write(
+                        held_queries.at[which, :, cols], queries_ref.at[device, head * 2 + which]
                     )
-        for read in reads:
-            read.start()
-        for read, write in zip(reads, writes):
-            read.wait()
-            write.start()
-        for write in writes:
-            write.wait()
+        for copy in reads:
+            copy.start()
+        for copy, following in zip(reads, writes):
+            copy.wait()
+            for later in following:
+                later.start()
+        for following in writes:
+            for later in following:
+                later.wait()
 
     copies = pairs * 2 + devices * heads * 2
     flat = pl.pallas_call(
@@ -89,9 +92,9 @@
         out_shape=[jax.ShapeDtypeStruct((devices, heads * 2, rows, part), query.dtype)]
         + [jax.ShapeDtypeStruct((2, block, HEAD_DIM), keys.dtype)] * pairs,
         scratch_shapes=[
-            pltpu.VMEM((pairs, 2, block, HEAD_DIM), keys.dtype),
-            pltpu.VMEM((devices, heads * 2, rows, part), query.dtype),
-            pltpu.SemaphoreType.DMA((copies,)),
+            pltpu.VMEM((count, 2, block, heads * HEAD_DIM), keys.dtype),
+            pltpu.VMEM((2, rows, width), query.dtype),
+            pltpu.SemaphoreType.DMA((count * 2 + 2,)),
             pltpu.SemaphoreType.DMA((copies,)),
         ],
         compiler_params=pltpu.CompilerParams(vmem_limit_bytes=VMEM_LIMIT),

time: 140 us -> 140 us (level)
  no operation moved by 1% of the time
where the time goes in v3:
time: 140 us; the launch traced here: 139 us
  Pallas kernels  56.8 us (41%)
  starting transfers between devices  43.7 us (31%)
  waiting for transfers between devices  35.4 us (25%)
  between operations  1.67 us (1%)
    pallas_call x2, Pallas kernels, attend(): pl.pallas_call(kernel, grid_spec=pltpu.PrefetchScalarGridSpec(num_scalar_...  45.1 us
    ppermute x15, starting transfers between devices, shifted(): lax.ppermute(value, axis, [(source, source + steps) for source in range(f...  33.6 us
    ppermute x15, waiting for transfers between devices, shifted(): lax.ppermute(value, axis, [(source, source + steps) for source in range(f...  32.7 us
    all_to_all x2, starting transfers between devices, exchanged(): return lax.all_to_all(value, axis, split_axis=0, concat_axis=0, tiled=True)  10.1 us
    pallas_call x2, Pallas kernels, finish(): pl.pallas_call(kernel, in_specs=[SMEM] * (3 + picks - 1) + [HBM] * (len(o...  7.45 us
    pallas_call x1, Pallas kernels, prepare(): pl.pallas_call(kernel, in_specs=[SMEM] * (1 + count) + [HBM] * 4, out_spe...  4.23 us
  transfers between devices with their start and end apart: 17, of which 9 were waited for; matrix products, arithmetic and copies ran while one was open for 0% of the time, Pallas kernels for 35%

profile of v3, /device:TPU:6, one launch (start us, length us, event | category | flops | bytes accessed | tf_op | source)
XLA Modules:
  0.0 138.8 jit_solution(14407603604762305158)
XLA Ops:
  3.2 2.4 %collective-permute-start = (s32[1,4]{1,0:T(1,128)}, s32[1,4]{1,0:T(1,128)S(1)}, u32[]{:S(2)}, u32[]{:S(2)}) collective-permute-start(s32[1,4]{1,0:T(1,128)} %chosen_ref.7), channel_id=1, source_target_pairs={{4,0},{8,4},{12,8},{16,12},{20,16},{24,20},{28,24},{5,1},{9,5},{13... | collective-permute-start | bytes 56 | tf_op jit(solution)/shard_map/ppermute | solution.py:25
  5.7 2.3 %collective-permute-done.2.refs_2_ = s32[1,4]{1,0:T(1,128)S(1)} collective-permute-done((s32[1,4]{1,0:T(1,128)}, s32[1,4]{1,0:T(1,128)S(1)}, u32[]{:S(2)}, u32[]{:S(2)}) %collective-permute-start.2) | collective-permute-done | bytes 48 | tf_op jit(solution)/shard_map/ppermute | solution.py:25
  8.1 1.6 %collective-permute-done.refs_0_ = s32[1,4]{1,0:T(1,128)S(1)} collective-permute-done((s32[1,4]{1,0:T(1,128)}, s32[1,4]{1,0:T(1,128)S(1)}, u32[]{:S(2)}, u32[]{:S(2)}) %collective-permute-start) | collective-permute-done | bytes 48 | tf_op jit(solution)/shard_map/ppermute | solution.py:25
  10.2 4.2 %prepare.1 = (bf16[4,4,128,512]{3,2,1,0:T(8,128)(2,1)}, bf16[2,512,128]{2,1,0:T(8,128)(2,1)}, bf16[2,512,128]{2,1,0:T(8,128)(2,1)}, bf16[2,512,128]{2,1,0:T(8,12...) custom-call(s32[1]{0:T(128)} %bitcast.seq_ref, ...), custom_call_target="tpu_custom_call" | custom-call | tf_op jit(solution)/shard_map/prepare/pallas_call | solution.py:88
  14.4 4.9 %all-to-all-start = ((bf16[4,4,128,512]{3,2,1,0:T(8,128)(2,1)}), bf16[4,4,128,512]{3,2,1,0:T(8,128)(2,1)}, u32[]{:S(2)}, u32[]{:S(2)}) async-start(bf16[4,4,128,512]{3,2,1,0:T(8,128)(2,1)} %get-tuple-element.38), calls=%async_computation | async-start | bytes 4194304 | tf_op jit(solution)/shard_map/all_to_all | solution.py:29
  19.4 3.4 %collective-permute-start.6 = (bf16[2,512,128]{2,1,0:T(8,128)(2,1)}, bf16[2,512,128]{2,1,0:T(8,128)(2,1)S(1)}, u32[]{:S(2)}, u32[]{:S(2)}) collective-permute-start(bf16[2,512,128]{2,1,0:T(8,128)(2,1)} %get-tuple-element.42), channel_id=1, source_target_pairs={{0,4},{4,8},{8,12},{12,16},{16,20},{20,24},{24,28},{1,5},{5,9},{9,... | collective-permute-start | bytes 786440 | tf_op jit(solution)/shard_map/ppermute | solution.py:25
  22.8 6.0 %collective-permute-start.7 = (bf16[2,512,128]{2,1,0:T(8,128)(2,1)}, bf16[2,512,128]{2,1,0:T(8,128)(2,1)}, u32[]{:S(2)}, u32[]{:S(2)}) collective-permute-start(bf16[2,512,128]{2,1,0:T(8,128)(2,1)} %get-tuple-element.43), channel_id=1, source_target_pairs={{0,8},{4,12},{8,16},{12,20},{16,24},{20,28},{1,9},{5,13},{9,17},{1... | collective-permute-start | bytes 786440 | tf_op jit(solution)/shard_map/ppermute | solution.py:25
  28.7 3.6 %collective-permute-start.8 = (bf16[2,512,128]{2,1,0:T(8,128)(2,1)}, bf16[2,512,128]{2,1,0:T(8,128)(2,1)}, u32[]{:S(2)}, u32[]{:S(2)}) collective-permute-start(bf16[2,512,128]{2,1,0:T(8,128)(2,1)} %get-tuple-element.44), channel_id=1, source_target_pairs={{0,12},{4,16},{8,20},{12,24},{16,28},{1,13},{5,17},{9,21},{13,25},... | collective-permute-start | bytes 786440 | tf_op jit(solution)/shard_map/ppermute | solution.py:25
  33.0 3.2 %collective-permute-start.3 = (bf16[2,512,128]{2,1,0:T(8,128)(2,1)}, bf16[2,512,128]{2,1,0:T(8,128)(2,1)S(1)}, u32[]{:S(2)}, u32[]{:S(2)}) collective-permute-start(bf16[2,512,128]{2,1,0:T(8,128)(2,1)} %get-tuple-element.39), channel_id=1, source_target_pairs={{0,4},{4,8},{8,12},{12,16},{16,20},{20,24},{24,28},{1,5},{5,9},{9,... | collective-permute-start | bytes 786440 | tf_op jit(solution)/shard_map/ppermute | solution.py:25
  36.1 1.3 collective-permute-start.4
  37.5 2.0 %collective-permute-start.5 = (bf16[2,512,128]{2,1,0:T(8,128)(2,1)}, bf16[2,512,128]{2,1,0:T(8,128)(2,1)}, u32[]{:S(2)}, u32[]{:S(2)}) collective-permute-start(bf16[2,512,128]{2,1,0:T(8,128)(2,1)} %get-tuple-element.41), channel_id=1, source_target_pairs={{0,12},{4,16},{8,20},{12,24},{16,28},{1,13},{5,17},{9,21},{13,25},... | collective-permute-start | bytes 786440 | tf_op jit(solution)/shard_map/ppermute | solution.py:25
  40.8 2.8 %all-to-all-done.queries_ref = bf16[4,4,128,512]{3,2,1,0:T(8,128)(2,1)} async-done(((bf16[4,4,128,512]{3,2,1,0:T(8,128)(2,1)}), bf16[4,4,128,512]{3,2,1,0:T(8,128)(2,1)}, u32[]{:S(2)}, u32[]{:S(2)}) %all-to-all-start) | async-done | bytes 2097184 | tf_op jit(solution)/shard_map/all_to_all | solution.py:29
  43.5 22.7 %attend.2 = (bf16[4,4,128,512]{3,2,1,0:T(8,128)(2,1)}, bf16[2,512,128]{2,1,0:T(8,128)(2,1)}, bf16[2,512,128]{2,1,0:T(8,128)(2,1)}, bf16[2,512,128]{2,1,0:T(8,128...) custom-call(s32[1,4]{1,0:T(1,128)} %chosen_ref.7, ...), custom_call_target="tpu_custom_call" | custom-call | flops 8053063680 | bytes 8388608 | tf_op jit(solution)/shard_map/attend/pallas_call | solution.py:226
  66.2 1.9 %collective-permute-start.9 = (bf16[2,512,128]{2,1,0:T(8,128)(2,1)}, bf16[2,512,128]{2,1,0:T(8,128)(2,1)S(1)}, u32[]{:S(2)}, u32[]{:S(2)}) collective-permute-start(bf16[2,512,128]{2,1,0:T(8,128)(2,1)} %get-tuple-element.53), channel_id=1, source_target_pairs={{4,0},{8,4},{12,8},{16,12},{20,16},{24,20},{28,24},{5,1},{9,5},{13... | collective-permute-start | bytes 786440 | tf_op jit(solution)/shard_map/ppermute | solution.py:25
  69.4 1.5 %collective-permute-start.11 = (bf16[2,512,128]{2,1,0:T(8,128)(2,1)}, bf16[2,512,128]{2,1,0:T(8,128)(2,1)}, u32[]{:S(2)}, u32[]{:S(2)}) collective-permute-start(bf16[2,512,128]{2,1,0:T(8,128)(2,1)} %get-tuple-element.55), channel_id=1, source_target_pairs={{12,0},{16,4},{20,8},{24,12},{28,16},{13,1},{17,5},{21,9},{25,13},... | collective-permute-start | bytes 786440 | tf_op jit(solution)/shard_map/ppermute | solution.py:25
  71.6 22.5 %attend.3 = (bf16[4,4,128,512]{3,2,1,0:T(8,128)(2,1)}, bf16[2,512,128]{2,1,0:T(8,128)(2,1)}, bf16[2,512,128]{2,1,0:T(8,128)(2,1)}, bf16[2,512,128]{2,1,0:T(8,128...) custom-call(s32[1,4]{1,0:T(1,128)} %chosen_ref.7, ...), custom_call_target="tpu_custom_call", output_to_operand_aliasing={{0}: (10, {})} | custom-call | flops 8053063680 | bytes 8388608 | tf_op jit(solution)/shard_map/attend/pallas_call | solution.py:226
  94.1 4.6 %collective-permute-done.11.refs_6_ = bf16[2,512,128]{2,1,0:T(8,128)(2,1)} collective-permute-done((bf16[2,512,128]{2,1,0:T(8,128)(2,1)}, bf16[2,512,128]{2,1,0:T(8,128)(2,1)}, u32[]{:S(2)}, u32[]{:S(2)}) %collective-permute-start.11) | collective-permute-done | bytes 262176 | tf_op jit(solution)/shard_map/ppermute | solution.py:25
  98.8 5.1 %all-to-all-start.1 = ((bf16[4,4,128,512]{3,2,1,0:T(8,128)(2,1)}), bf16[4,4,128,512]{3,2,1,0:T(8,128)(2,1)}, u32[]{:S(2)}, u32[]{:S(2)}) async-start(bf16[4,4,128,512]{3,2,1,0:T(8,128)(2,1)} %get-tuple-element.57), calls=%async_computation.1 | async-start | bytes 4194304 | tf_op jit(solution)/shard_map/all_to_all | solution.py:29
  103.9 1.9 %collective-permute-start.12 = (bf16[2,512,128]{2,1,0:T(8,128)(2,1)}, bf16[2,512,128]{2,1,0:T(8,128)(2,1)S(1)}, u32[]{:S(2)}, u32[]{:S(2)}) collective-permute-start(bf16[2,512,128]{2,1,0:T(8,128)(2,1)} %get-tuple-element.59), channel_id=1, source_target_pairs={{4,0},{8,4},{12,8},{16,12},{20,16},{24,20},{28,24},{5,1},{9,5},{13... | collective-permute-start | bytes 786440 | tf_op jit(solution)/shard_map/ppermute | solution.py:25
  108.4 3.2 %finish.2 = (bf16[16384,256]{1,0:T(8,128)(2,1)}, bf16[16384,256]{1,0:T(8,128)(2,1)}) custom-call(s32[1]{0:T(128)} %bitcast.seq_ref, s32[1,4]{1,0:T(1,128)} %chosen_ref.7, s32[1]{0:T(128)S(6)} %copy.20.pos_ref, s32[1,4]{1,0:T(1,128)} %copy-done.8, s32[1,4]{1,0:T(1,128)} %copy-done.7, ...), custom_call_target="tpu_custom_call", output_to_operand_aliasing={{0}: (11, {}), {1}: (12, {})} | custom-call | tf_op jit(solution)/shard_map/finish/pallas_call | solution.py:355
  111.6 4.4 %collective-permute-done.12.refs_5_ = bf16[2,512,128]{2,1,0:T(8,128)(2,1)S(1)} collective-permute-done((bf16[2,512,128]{2,1,0:T(8,128)(2,1)}, bf16[2,512,128]{2,1,0:T(8,128)(2,1)S(1)}, u32[]{:S(2)}, u32[]{:S(2)}) %collective-permute-start.12) | collective-permute-done | bytes 262176 | tf_op jit(solution)/shard_map/ppermute | solution.py:25
  116.0 1.4 %collective-permute-done.13.refs_6_ = bf16[2,512,128]{2,1,0:T(8,128)(2,1)S(1)} collective-permute-done((bf16[2,512,128]{2,1,0:T(8,128)(2,1)}, bf16[2,512,128]{2,1,0:T(8,128)(2,1)S(1)}, u32[]{:S(2)}, u32[]{:S(2)}) %collective-permute-start.13) | collective-permute-done | bytes 262176 | tf_op jit(solution)/shard_map/ppermute | solution.py:25
  117.5 16.9 %collective-permute-done.14.refs_7_ = bf16[2,512,128]{2,1,0:T(8,128)(2,1)} collective-permute-done((bf16[2,512,128]{2,1,0:T(8,128)(2,1)}, bf16[2,512,128]{2,1,0:T(8,128)(2,1)}, u32[]{:S(2)}, u32[]{:S(2)}) %collective-permute-start.14) | collective-permute-done | bytes 262176 | tf_op jit(solution)/shard_map/ppermute | solution.py:25
  134.3 4.3 %finish.3 = (bf16[128,4096]{1,0:T(8,128)(2,1)}, bf16[128,4096]{1,0:T(8,128)(2,1)}, bf16[16384,256]{1,0:T(8,128)(2,1)}, bf16[16384,256]{1,0:T(8,128)(2,1)}) custom-call(s32[1]{0:T(128)} %bitcast.seq_ref, s32[1,4]{1,0:T(1,128)} %chosen_ref.7, s32[1]{0:T(128)S(6)} %copy.20.pos_ref, s32[1,4]{1,0:T(1,128)} %copy-done.8, ...), custom_call_target="tpu_custom_call", output_to_operand_aliasing={{2}: (12, {}), {3}: (13, {})} | custom-call | tf_op jit(solution)/shard_map/finish/pallas_call | solution.py:355
  (33 shorter events, 9.1 us)
Async XLA Ops:
  0.6 7.4 %collective-permute-start.2 = (s32[1,4]{1,0:T(1,128)}, s32[1,4]{1,0:T(1,128)S(1)}, u32[]{:S(2)}, u32[]{:S(2)}) collective-permute-start(s32[1,4]{1,0:T(1,128)} %chosen_ref.7), channel_id=1, source_target_pairs={{12,0},{16,4},{20,8},{24,12},{28,16},{13,1},{17,5},{21,9},{25,13},... | collective-permute-start | bytes 56 | tf_op jit(solution)/shard_map/ppermute | solution.py:25
  1.9 6.2 %collective-permute-start.1 = (s32[1,4]{1,0:T(1,128)}, s32[1,4]{1,0:T(1,128)S(1)}, u32[]{:S(2)}, u32[]{:S(2)}) collective-permute-start(s32[1,4]{1,0:T(1,128)} %chosen_ref.7), channel_id=1, source_target_pairs={{8,0},{12,4},{16,8},{20,12},{24,16},{28,20},{9,1},{13,5},{17,9},{2... | collective-permute-start | bytes 56 | tf_op jit(solution)/shard_map/ppermute | solution.py:25
  3.2 6.5 %collective-permute-start = (s32[1,4]{1,0:T(1,128)}, s32[1,4]{1,0:T(1,128)S(1)}, u32[]{:S(2)}, u32[]{:S(2)}) collective-permute-start(s32[1,4]{1,0:T(1,128)} %chosen_ref.7), channel_id=1, source_target_pairs={{4,0},{8,4},{12,8},{16,12},{20,16},{24,20},{28,24},{5,1},{9,5},{13... | collective-permute-start | bytes 56 | tf_op jit(solution)/shard_map/ppermute | solution.py:25
  8.0 1.7 %copy-start.6 = (s32[1,4]{1,0:T(1,128)}, s32[1,4]{1,0:T(1,128)S(1)}, u32[]{:S(2)}) copy-start(s32[1,4]{1,0:T(1,128)S(1)} %collective-permute-done.2.refs_2_) | copy-start | bytes 52
  8.1 1.6 %copy-start.7 = (s32[1,4]{1,0:T(1,128)}, s32[1,4]{1,0:T(1,128)S(1)}, u32[]{:S(2)}) copy-start(s32[1,4]{1,0:T(1,128)S(1)} %collective-permute-done.1.refs_1_) | copy-start | bytes 52
  14.4 29.1 %all-to-all-start = ((bf16[4,4,128,512]{3,2,1,0:T(8,128)(2,1)}), bf16[4,4,128,512]{3,2,1,0:T(8,128)(2,1)}, u32[]{:S(2)}, u32[]{:S(2)}) async-start(bf16[4,4,128,512]{3,2,1,0:T(8,128)(2,1)} %get-tuple-element.38), calls=%async_computation | async-start | bytes 4194304 | tf_op jit(solution)/shard_map/all_to_all | solution.py:29
  19.4 18.1 %collective-permute-start.6 = (bf16[2,512,128]{2,1,0:T(8,128)(2,1)}, bf16[2,512,128]{2,1,0:T(8,128)(2,1)S(1)}, u32[]{:S(2)}, u32[]{:S(2)}) collective-permute-start(bf16[2,512,128]{2,1,0:T(8,128)(2,1)} %get-tuple-element.42), channel_id=1, source_target_pairs={{0,4},{4,8},{8,12},{12,16},{16,20},{20,24},{24,28},{1,5},{5,9},{9,... | collective-permute-start | bytes 786440 | tf_op jit(solution)/shard_map/ppermute | solution.py:25
  22.8 16.7 %collective-permute-start.7 = (bf16[2,512,128]{2,1,0:T(8,128)(2,1)}, bf16[2,512,128]{2,1,0:T(8,128)(2,1)}, u32[]{:S(2)}, u32[]{:S(2)}) collective-permute-start(bf16[2,512,128]{2,1,0:T(8,128)(2,1)} %get-tuple-element.43), channel_id=1, source_target_pairs={{0,8},{4,12},{8,16},{12,20},{16,24},{20,28},{1,9},{5,13},{9,17},{1... | collective-permute-start | bytes 786440 | tf_op jit(solution)/shard_map/ppermute | solution.py:25
  28.7 12.0 %collective-permute-start.8 = (bf16[2,512,128]{2,1,0:T(8,128)(2,1)}, bf16[2,512,128]{2,1,0:T(8,128)(2,1)}, u32[]{:S(2)}, u32[]{:S(2)}) collective-permute-start(bf16[2,512,128]{2,1,0:T(8,128)(2,1)} %get-tuple-element.44), channel_id=1, source_target_pairs={{0,12},{4,16},{8,20},{12,24},{16,28},{1,13},{5,17},{9,21},{13,25},... | collective-permute-start | bytes 786440 | tf_op jit(solution)/shard_map/ppermute | solution.py:25
  33.0 36.5 %collective-permute-start.3 = (bf16[2,512,128]{2,1,0:T(8,128)(2,1)}, bf16[2,512,128]{2,1,0:T(8,128)(2,1)S(1)}, u32[]{:S(2)}, u32[]{:S(2)}) collective-permute-start(bf16[2,512,128]{2,1,0:T(8,128)(2,1)} %get-tuple-element.39), channel_id=1, source_target_pairs={{0,4},{4,8},{8,12},{12,16},{16,20},{20,24},{24,28},{1,5},{5,9},{9,... | collective-permute-start | bytes 786440 | tf_op jit(solution)/shard_map/ppermute | solution.py:25
  36.1 34.8 %collective-permute-start.4 = (bf16[2,512,128]{2,1,0:T(8,128)(2,1)}, bf16[2,512,128]{2,1,0:T(8,128)(2,1)S(1)}, u32[]{:S(2)}, u32[]{:S(2)}) collective-permute-start(bf16[2,512,128]{2,1,0:T(8,128)(2,1)} %get-tuple-element.40), channel_id=1, source_target_pairs={{0,8},{4,12},{8,16},{12,20},{16,24},{20,28},{1,9},{5,13},{9,17},{1... | collective-permute-start | bytes 786440 | tf_op jit(solution)/shard_map/ppermute | solution.py:25
  37.5 6.1 %copy-start.4 = (bf16[2,512,128]{2,1,0:T(8,128)(2,1)}, bf16[2,512,128]{2,1,0:T(8,128)(2,1)S(1)}, u32[]{:S(2)}) copy-start(bf16[2,512,128]{2,1,0:T(8,128)(2,1)S(1)} %collective-permute-done.6.refs_4_) | copy-start | bytes 786436
  37.5 33.5 %collective-permute-start.5 = (bf16[2,512,128]{2,1,0:T(8,128)(2,1)}, bf16[2,512,128]{2,1,0:T(8,128)(2,1)}, u32[]{:S(2)}, u32[]{:S(2)}) collective-permute-start(bf16[2,512,128]{2,1,0:T(8,128)(2,1)} %get-tuple-element.41), channel_id=1, source_target_pairs={{0,12},{4,16},{8,20},{12,24},{16,28},{1,13},{5,17},{9,21},{13,25},... | collective-permute-start | bytes 786440 | tf_op jit(solution)/shard_map/ppermute | solution.py:25
  66.2 27.9 %collective-permute-start.9 = (bf16[2,512,128]{2,1,0:T(8,128)(2,1)}, bf16[2,512,128]{2,1,0:T(8,128)(2,1)S(1)}, u32[]{:S(2)}, u32[]{:S(2)}) collective-permute-start(bf16[2,512,128]{2,1,0:T(8,128)(2,1)} %get-tuple-element.53), channel_id=1, source_target_pairs={{4,0},{8,4},{12,8},{16,12},{20,16},{24,20},{28,24},{5,1},{9,5},{13... | collective-permute-start | bytes 786440 | tf_op jit(solution)/shard_map/ppermute | solution.py:25
  68.1 26.0 %collective-permute-start.10 = (bf16[2,512,128]{2,1,0:T(8,128)(2,1)}, bf16[2,512,128]{2,1,0:T(8,128)(2,1)}, u32[]{:S(2)}, u32[]{:S(2)}) collective-permute-start(bf16[2,512,128]{2,1,0:T(8,128)(2,1)} %get-tuple-element.54), channel_id=1, source_target_pairs={{8,0},{12,4},{16,8},{20,12},{24,16},{28,20},{9,1},{13,5},{17,9},{2... | collective-permute-start | bytes 786440 | tf_op jit(solution)/shard_map/ppermute | solution.py:25
  69.4 1.5 %copy-start = (bf16[2,512,128]{2,1,0:T(8,128)(2,1)}, bf16[2,512,128]{2,1,0:T(8,128)(2,1)S(1)}, u32[]{:S(2)}) copy-start(bf16[2,512,128]{2,1,0:T(8,128)(2,1)S(1)} %collective-permute-done.3.refs_4_) | copy-start | bytes 786436
  69.4 29.3 %collective-permute-start.11 = (bf16[2,512,128]{2,1,0:T(8,128)(2,1)}, bf16[2,512,128]{2,1,0:T(8,128)(2,1)}, u32[]{:S(2)}, u32[]{:S(2)}) collective-permute-start(bf16[2,512,128]{2,1,0:T(8,128)(2,1)} %get-tuple-element.55), channel_id=1, source_target_pairs={{12,0},{16,4},{20,8},{24,12},{28,16},{13,1},{17,5},{21,9},{25,13},... | collective-permute-start | bytes 786440 | tf_op jit(solution)/shard_map/ppermute | solution.py:25
  94.1 14.3 %copy-start.1 = (bf16[2,512,128]{2,1,0:T(8,128)(2,1)}, bf16[2,512,128]{2,1,0:T(8,128)(2,1)S(1)}, u32[]{:S(2)}) copy-start(bf16[2,512,128]{2,1,0:T(8,128)(2,1)S(1)} %collective-permute-done.9.refs_4_) | copy-start | bytes 786436
  98.8 35.6 %all-to-all-start.1 = ((bf16[4,4,128,512]{3,2,1,0:T(8,128)(2,1)}), bf16[4,4,128,512]{3,2,1,0:T(8,128)(2,1)}, u32[]{:S(2)}, u32[]{:S(2)}) async-start(bf16[4,4,128,512]{3,2,1,0:T(8,128)(2,1)} %get-tuple-element.57), calls=%async_computation.1 | async-start | bytes 4194304 | tf_op jit(solution)/shard_map/all_to_all | solution.py:29
  103.9 12.1 %collective-permute-start.12 = (bf16[2,512,128]{2,1,0:T(8,128)(2,1)}, bf16[2,512,128]{2,1,0:T(8,128)(2,1)S(1)}, u32[]{:S(2)}, u32[]{:S(2)}) collective-permute-start(bf16[2,512,128]{2,1,0:T(8,128)(2,1)} %get-tuple-element.59), channel_id=1, source_target_pairs={{4,0},{8,4},{12,8},{16,12},{20,16},{24,20},{28,24},{5,1},{9,5},{13... | collective-permute-start | bytes 786440 | tf_op jit(solution)/shard_map/ppermute | solution.py:25
  105.8 11.6 %collective-permute-start.13 = (bf16[2,512,128]{2,1,0:T(8,128)(2,1)}, bf16[2,512,128]{2,1,0:T(8,128)(2,1)S(1)}, u32[]{:S(2)}, u32[]{:S(2)}) collective-permute-start(bf16[2,512,128]{2,1,0:T(8,128)(2,1)} %get-tuple-element.60), channel_id=1, source_target_pairs={{8,0},{12,4},{16,8},{20,12},{24,16},{28,20},{9,1},{13,5},{17,9},{2... | collective-permute-start | bytes 786440 | tf_op jit(solution)/shard_map/ppermute | solution.py:25
  107.1 27.2 %collective-permute-start.14 = (bf16[2,512,128]{2,1,0:T(8,128)(2,1)}, bf16[2,512,128]{2,1,0:T(8,128)(2,1)}, u32[]{:S(2)}, u32[]{:S(2)}) collective-permute-start(bf16[2,512,128]{2,1,0:T(8,128)(2,1)} %get-tuple-element.61), channel_id=1, source_target_pairs={{12,0},{16,4},{20,8},{24,12},{28,16},{13,1},{17,5},{21,9},{25,13},... | collective-permute-start | bytes 786440 | tf_op jit(solution)/shard_map/ppermute | solution.py:25
  116.0 18.3 %copy-start.3 = (bf16[2,512,128]{2,1,0:T(8,128)(2,1)}, bf16[2,512,128]{2,1,0:T(8,128)(2,1)S(1)}, u32[]{:S(2)}) copy-start(bf16[2,512,128]{2,1,0:T(8,128)(2,1)S(1)} %collective-permute-done.12.refs_5_) | copy-start | bytes 786436
  117.5 16.9 %copy-start.5 = (bf16[2,512,128]{2,1,0:T(8,128)(2,1)}, bf16[2,512,128]{2,1,0:T(8,128)(2,1)S(1)}, u32[]{:S(2)}) copy-start(bf16[2,512,128]{2,1,0:T(8,128)(2,1)S(1)} %collective-permute-done.13.refs_6_) | copy-start | bytes 786436
  (2 other events, 1.2 us)
